TPU v7x, 128 devices: a whole 4x4x4 slice. The times are simulated.
128 devices in a mesh: row: 32 (over z, y_hi, x), col: 4 (over y_lo, core).
Axes of the slice: x: 4, y: 4 (y_hi: 2, y_lo: 2; y = y_hi * 2 + y_lo), z: 4, core: 2. Of those that a mesh axis runs over, the one named last changes fastest.
Arguments:
- pair_map: bfloat16 [704, 704, 128], P('row', 'col'), may hold values from -40 to 40, as said below
- in_gain: float32 [128], replicated, may hold values from 0.1 to 1.9
- project_weight: bfloat16 [128, 512], replicated, may hold values from -0.5 to 0.5
- gate_weight: bfloat16 [128, 128], replicated, may hold values from -0.5 to 0.5
- out_gain: float32 [128], replicated, may hold values from 0.1 to 1.9
- out_weight: bfloat16 [128, 128], replicated, may hold values from -0.5 to 0.5
Outputs:
- update_t: bfloat16 [704, 704, 128], P('row', 'col')
Inputs may be any that keep to these rules, and one draw needn't show every extreme that they name: `pair_map`: pair features.
All inputs are finite; a program needn't handle non-finite values.
Results may differ from a plain program's by a relative error of at most 0.019.
Values may be sent and summed in bfloat16 or wider, within the bound.
A program may use at most 192 MiB of HBM per device.

v0:
```python
import jax
import jax.numpy as jnp
from jax import lax
from jax.sharding import PartitionSpec as P


def layer_norm(values, gain):
    values = values.astype(jnp.float32)
    center = values - jnp.mean(values, axis=-1, keepdims=True)
    spread = jnp.mean(center * center, axis=-1, keepdims=True)
    return center * lax.rsqrt(spread + 1e-05) * gain


def finish(products, normed_pairs, gate_weight, out_gain, out_weight):
    row_count, column_count, channels = products.shape
    width = out_weight.shape[1]
    hidden = layer_norm(products.reshape(row_count * column_count, channels), out_gain).astype(
        jnp.bfloat16
    )
    flat_pairs = normed_pairs.reshape(row_count * column_count, width)
    gate = jax.nn.sigmoid(jnp.dot(flat_pairs, gate_weight, preferred_element_type=jnp.float32))
    mixed = gate * jnp.dot(hidden, out_weight, preferred_element_type=jnp.float32)
    return mixed.astype(jnp.bfloat16).reshape(row_count, column_count, width)


def swap_indices(block):
    spread_out = lax.all_to_all(block, "col", split_axis=2, concat_axis=1, tiled=True)
    crossed = lax.all_to_all(
        lax.all_to_all(spread_out, "row", split_axis=1, concat_axis=0, tiled=True),
        "col",
        split_axis=0,
        concat_axis=2,
        tiled=True,
    )
    return jnp.transpose(crossed, (1, 0, 2))


def body(pair_map, in_gain, project_weight, gate_weight, out_gain, out_weight):
    row_count, column_count, width = pair_map.shape
    channels = out_weight.shape[0]
    normed_flat = layer_norm(pair_map.reshape(row_count * column_count, width), in_gain).astype(
        jnp.bfloat16
    )
    projected = jnp.dot(normed_flat, project_weight, preferred_element_type=jnp.float32)
    left_factor = (
        jax.nn.sigmoid(projected[:, :channels]) * projected[:, channels : 2 * channels]
    ).astype(jnp.bfloat16)
    right_factor = (
        jax.nn.sigmoid(projected[:, 2 * channels : 3 * channels]) * projected[:, 3 * channels :]
    ).astype(jnp.bfloat16)
    left_factor = left_factor.reshape(row_count, column_count, channels)
    right_factor = right_factor.reshape(row_count, column_count, channels)
    normed_pairs = normed_flat.reshape(row_count, column_count, width)
    partial_sums = jnp.einsum(
        "ikc,jkc->ijc",
        left_factor,
        lax.all_gather(right_factor, "row", axis=0, tiled=True),
        preferred_element_type=jnp.float32,
    )
    products = lax.psum_scatter(
        partial_sums.astype(jnp.bfloat16), "col", scatter_dimension=1, tiled=True
    ).astype(jnp.float32)
    update = finish(products, normed_pairs, gate_weight, out_gain, out_weight)
    return swap_indices(update)


def solution(mesh):
    return jax.shard_map(
        body,
        mesh=mesh,
        in_specs=(P("row", "col", None), P(), P(), P(), P(), P()),
        out_specs=P("row", "col", None),
        check_vma=False,
    )
```

profile of v0, /device:TPU:1, one launch (start us, length us, event | category | flops | bytes accessed | tf_op | source)
XLA Modules:
  0.0 523.2 jit_solution(11426100945860450406)
XLA Ops:
  6.5 1.8 convert_reduce_fusion
  8.3 2.6 multiply_reduce_fusion.1
  11.1 2.0 fusion.17
  14.4 2.3 fusion.4
  16.9 2.1 copy.18
  19.1 248.3 %all-gather.2.cloned.1.call-done = bf16[704,176,128]{2,1,0:T(8,128)(2,1)} async-done(((bf16[22,176,128]{2,1,0:T(8,128)(2,1)}), bf16[704,176,128]{2,1,0:T(8,128)(2,1)}) %all-gather.2.cloned.1.call-update) | async-done | bytes 31719440 | tf_op jit(solution)/shard_map/all_gather | solution.py:57
  267.3 62.9 %copy.17 = bf16[704,176,128]{1,0,2:T(8,128)(2,1)} copy(bf16[704,176,128]{2,1,0:T(8,128)(2,1)} %all-gather.2.cloned.1.call-done) | data formatting | bytes 63438848 | tf_op jit(solution)/shard_map/all_gather | solution.py:57
  330.2 20.2 %convert_bitcast_fusion = bf16[22,704,128]{1,0,2:T(8,128)(2,1)} fusion(bf16[704,176,128]{1,0,2:T(8,128)(2,1)} %copy.17, bf16[22,176,128]{1,0,2:T(8,128)(2,1)S(1)} %copy.18), kind=kOutput, calls=%fused_computation.6 | convolution fusion | flops 699809792 | bytes 36675584 | tf_op jit(solution)/shard_map/ikc,jkc->ijc/dot_general | solution.py:54
  350.4 7.3 %copy.19 = bf16[22,704,128]{2,0,1:T(8,128)(2,1)} copy(bf16[22,704,128]{1,0,2:T(8,128)(2,1)} %convert_bitcast_fusion) | data formatting | bytes 7929856 | tf_op jit(solution)/shard_map/convert_element_type | solution.py:61
  358.5 1.9 fusion.2
  360.4 42.3 %reduce-scatter.2.cloned.1.call-done = bf16[22,176,128]{2,0,1:T(8,128)(2,1)} async-done(((bf16[22,704,128]{2,0,1:T(8,128)(2,1)}), bf16[22,176,128]{2,0,1:T(8,128)(2,1)}) %reduce-scatter.2.cloned.1.call-update) | async-done | bytes 991248 | tf_op jit(solution)/shard_map/reduce_scatter | solution.py:60
  402.7 2.1 fusion.18
  405.0 2.6 multiply_reduce_fusion
  407.9 2.2 fusion.14
  411.8 21.9 %all_to_all.54 = bf16[22,176,128]{1,0,2:T(8,128)(2,1)S(1)} all-to-all(bf16[22,176,128]{1,0,2:T(8,128)(2,1)S(1)} %copy.21), channel_id=1, replica_groups=mesh['row'=32,'col'=4] {'col'}, dimensions={2} | all-to-all | bytes 1982464 | tf_op jit(solution)/shard_map/all_to_all | solution.py:27
  433.7 4.1 copy.32
  437.7 6.3 %reshape.86 = bf16[32,2,7744]{2,1,0:T(2,128)(2,1)S(1)} reshape(bf16[704,22,32]{2,1,0:T(8,128)(2,1)} %bitcast.45) | data formatting | bytes 1982464
  444.1 24.7 %all_to_all.55 = bf16[32,2,7744]{2,1,0:T(2,128)(2,1)S(1)} all-to-all(bf16[32,2,7744]{2,1,0:T(2,128)(2,1)S(1)} %reshape.86), channel_id=1, replica_groups=mesh['row'=32,'col'=4] {'row'}, dimensions={0} | all-to-all | bytes 1982464 | tf_op jit(solution)/shard_map/all_to_all | solution.py:29
  468.8 5.2 reshape.87
  473.9 4.9 copy.35
  478.8 5.0 reshape.88
  483.8 18.2 %all_to_all.56 = bf16[4,2,61952]{2,1,0:T(2,128)(2,1)S(1)} all-to-all(bf16[4,2,61952]{2,1,0:T(2,128)(2,1)S(1)} %reshape.88), channel_id=1, replica_groups=mesh['row'=32,'col'=4] {'col'}, dimensions={0} | all-to-all | bytes 1982464 | tf_op jit(solution)/shard_map/all_to_all | solution.py:28
  502.0 5.4 %reshape.89 = bf16[704,22,32]{2,1,0:T(8,128)(2,1)} reshape(bf16[4,2,61952]{2,1,0:T(2,128)(2,1)S(1)} %all_to_all.56) | data formatting | bytes 1982464
  507.5 7.1 %copy.36 = bf16[4,176,22,32]{1,0,3,2:T(4,128)(2,1)S(1)} copy(bf16[4,176,22,32]{3,2,1,0:T(8,128)(2,1)} %bitcast.48) | data formatting | bytes 1982464 | tf_op jit(solution)/shard_map/all_to_all | solution.py:28
  (36 shorter events, 6.1 us)
Async XLA Ops:
  6.5 6.6 %copy-start = (bf16[128,512]{1,0:T(8,128)(2,1)S(1)}, bf16[128,512]{1,0:T(8,128)(2,1)}, u32[]{:S(2)}) copy-start(bf16[128,512]{1,0:T(8,128)(2,1)} %param.8) | copy-start | bytes 393220
  6.5 4.6 copy-start.3
  6.5 4.6 copy-start.6
  6.5 260.8 %all-gather.2.cloned.1.call-start = ((), (), s32[]{:S(2)}) async-start(), calls=%async_computation.4 | async-start | bytes 32710656 | tf_op jit(solution)/shard_map/all_gather | solution.py:57
  16.7 386.0 %reduce-scatter.2.cloned.1.call-start = ((), (), s32[]{:S(2)}) async-start(), calls=%async_computation.5 | async-start | bytes 5406720 | tf_op jit(solution)/shard_map/reduce_scatter | solution.py:60
  357.7 0.8 copy-start.8
  402.7 5.0 copy-start.2
  405.0 2.9 copy-start.7
  407.9 2.2 copy-start.4
  407.9 2.2 copy-start.5
  514.6 1.8 copy-start.1
Sparse Core Ops, SparseCore 0:
  16.8 250.4 all-gather.1
  357.9 44.7 reduce-scatter.1
where the time goes:
time: 525 us; the launch traced here: 523 us
  waiting for transfers between devices  291 us (55%)
  local copies, waits for them, and re-layouts  114 us (22%)
  blocking collectives  64.8 us (12%)
  matrix products  23.8 us (5%)
  other arithmetic  15.8 us (3%)
  between operations  13.7 us (3%)
    all_gather x1, waiting for transfers between devices, body(): lax.all_gather(right_factor, 'row', axis=0, tiled=True)  248 us
    all_gather x1, local copies, waits for them, and re-layouts, body(): lax.all_gather(right_factor, 'row', axis=0, tiled=True)  62.9 us
    reduce_scatter x1, waiting for transfers between devices, body(): lax.psum_scatter(partial_sums.astype(jnp.bfloat16), 'col', scatter_dimens...  42.3 us
    all_to_all x1, blocking collectives, swap_indices(): lax.all_to_all(spread_out, 'row', split_axis=1, concat_axis=0, tiled=True)  24.7 us
    unnamed x22, local copies, waits for them, and re-layouts  22.7 us
    all_to_all x1, blocking collectives, swap_indices(): lax.all_to_all(block, 'col', split_axis=2, concat_axis=1, tiled=True)  21.9 us
    dot_general x1, matrix products, body(): jnp.einsum('ikc,jkc->ijc', left_factor, lax.all_gather(right_factor, 'row...  20.2 us
    all_to_all x1, blocking collectives, swap_indices(): lax.all_to_all(lax.all_to_all(spread_out, 'row', split_axis=1, concat_axi...  18.2 us
  transfers between devices with their start and end apart: 2, of which 2 were waited for; matrix products, arithmetic and copies ran while one was open for 1% of the time, Pallas kernels for 0%

commit v1 on v0

v1 whole, which is shorter than its diff:
```python
import functools

import jax
import jax.numpy as jnp
from jax import lax
from jax.experimental import pallas as pl
from jax.experimental.pallas import tpu as pltpu
from jax.sharding import PartitionSpec as P

MESH = pl.DeviceIdType.MESH
F32 = jnp.float32
BF16 = jnp.bfloat16
VMEM_LIMIT = 56 * 2**20

ROWS = 22
ROWS_PAD = 24
COLS = 176
CHANNELS = 128
HALF = 64
LANES = 384
BLOCKS = 32
NT = (((1,), (1,)), ((), ()))
TN = (((0,), (0,)), ((), ()))


def sigmoid(x):
    return 0.5 * jnp.tanh(0.5 * x) + 0.5


def place():
    row = lax.axis_index("row")
    col = lax.axis_index("col")
    return row, col


def chip_at(row, col, step):
    z, y, x = row // 8, ((row // 4) % 2) * 2 + col // 2, row % 4
    walk = (step * 37) % 64
    z, y, x = (z + walk // 16) % 4, (y + (walk // 4) % 4) % 4, (x + walk % 4) % 4
    row2 = z * 8 + (y // 2) * 4 + x
    low = y % 2
    return {"row": row2, "col": low * 2 + col % 2}, row2 * 2 + low


def project_kernel(own_ref, sib_ref, gain_ref, weight_ref, lr_ref, g_ref, wt, normed, lr32, g32):
    half = lax.axis_index("col") % 2
    wt[...] = weight_ref[...].astype(F32).T
    parts = [wt[pl.ds(pl.multiple_of(128 * n + HALF * half, HALF), HALF), :] for n in range(4)]
    weight = jnp.concatenate(parts, axis=0).astype(BF16)
    ones = jnp.full((128, 128), 1.0 / 128, BF16)
    normed[2 * COLS :, :] = jnp.zeros((LANES - 2 * COLS, 128), BF16)
    for pad in (22, 23, 46, 47):
        for t in range(3):
            lr32[t, pl.ds(pad, HALF, stride=48), :] = jnp.zeros((HALF, 128), F32)
    for pad in (22, 23):
        g32[pl.ds(pad, COLS, stride=ROWS_PAD), :] = jnp.zeros((COLS, 128), F32)

    @pl.loop(0, ROWS)
    def _(i):
        for n, ref in enumerate((own_ref, sib_ref)):
            x = ref[i]
            center = x.astype(F32) - jnp.dot(x, ones, preferred_element_type=F32)
            spread = jnp.dot((center * center).astype(BF16), ones, preferred_element_type=F32)
            y = (center * lax.rsqrt(spread + 1e-05) * gain_ref[...]).astype(BF16)
            normed[n * COLS : (n + 1) * COLS, :] = y
            if n == 0:
                g32[pl.ds(i, COLS, stride=ROWS_PAD), :] = y.astype(F32)
        projected = lax.dot_general(weight, normed[...], NT, preferred_element_type=F32)
        left = sigmoid(projected[0:64]) * projected[64:128]
        right = sigmoid(projected[128:192]) * projected[192:256]
        for t in range(3):
            tile = slice(128 * t, 128 * (t + 1))
            lr32[t, pl.ds(i, HALF, stride=48), :] = left[:, tile]
            lr32[t, pl.ds(24 + i, HALF, stride=48), :] = right[:, tile]

    @pl.loop(0, HALF)
    def _(c):
        rows = pl.ds(pl.multiple_of(c * 48, 48), 48)
        for t in range(3):
            lr_ref[c, :, 128 * t : 128 * (t + 1)] = lr32[t, rows, :].astype(BF16)

    @pl.loop(0, COLS)
    def _(j):
        g_ref[j] = g32[pl.ds(pl.multiple_of(j * ROWS_PAD, ROWS_PAD), ROWS_PAD), :].astype(BF16)


def project(own, sib, gain, weight):
    return pl.pallas_call(
        project_kernel,
        out_shape=(
            jax.ShapeDtypeStruct((HALF, 48, LANES), BF16),
            jax.ShapeDtypeStruct((COLS, ROWS_PAD, 128), BF16),
        ),
        in_specs=[pl.BlockSpec(memory_space=pltpu.VMEM)] * 4,
        out_specs=[pl.BlockSpec(memory_space=pltpu.VMEM)] * 2,
        scratch_shapes=[
            pltpu.VMEM((512, 128), F32),
            pltpu.VMEM((LANES, 128), BF16),
            pltpu.VMEM((3, HALF * 48, 128), F32),
            pltpu.VMEM((COLS * ROWS_PAD, 128), F32),
        ],
        compiler_params=pltpu.CompilerParams(vmem_limit_bytes=VMEM_LIMIT),
        name="project",
    )(own, sib, gain, weight)


def exchange_kernel(src_ref, dst_ref, send, recv, local):
    row, col = place()
    me = row * 2 + col // 2
    barrier = pltpu.get_barrier_semaphore()

    @pl.loop(1, 64)
    def _(s):
        device, _ = chip_at(row, col, s)
        pl.semaphore_signal(barrier, inc=1, device_id=device, device_id_type=MESH)

    own = pltpu.make_async_copy(src_ref.at[me], dst_ref.at[me], local)
    own.start()
    pl.semaphore_wait(barrier, 63)

    def copy(s):
        device, chip = chip_at(row, col, s)
        return pltpu.make_async_remote_copy(
            src_ref=src_ref.at[chip],
            dst_ref=dst_ref.at[me],
            send_sem=send.at[s],
            recv_sem=recv.at[s],
            device_id=device,
            device_id_type=MESH,
        )

    @pl.loop(1, 64)
    def _(s):
        copy(s).start()

    own.wait()

    @pl.loop(1, 64)
    def _(s):
        copy(s).wait()


def exchange(x, collective_id, name):
    return pl.pallas_call(
        exchange_kernel,
        out_shape=jax.ShapeDtypeStruct(x.shape, x.dtype),
        in_specs=[pl.BlockSpec(memory_space=pltpu.VMEM)],
        out_specs=pl.BlockSpec(memory_space=pltpu.VMEM),
        scratch_shapes=[
            pltpu.SemaphoreType.DMA((64,)),
            pltpu.SemaphoreType.DMA((64,)),
            pltpu.SemaphoreType.DMA,
        ],
        compiler_params=pltpu.CompilerParams(
            collective_id=collective_id, has_side_effects=True, vmem_limit_bytes=VMEM_LIMIT
        ),
        name=name,
    )(x)


def triangle_kernel(x_ref, out_ref, left, right):
    @pl.loop(0, BLOCKS // 2)
    def _(b):
        for low in range(2):
            one = x_ref[4 * b + low].astype(F32)
            two = x_ref[4 * b + 2 + low].astype(F32)
            rows = pl.ds(pl.multiple_of(48 * b, 48), 48)
            lanes = slice(LANES * low, LANES * (low + 1))
            left[rows, lanes] = jnp.concatenate([one[:24], two[:24]], axis=0).astype(BF16)
            right[rows, lanes] = jnp.concatenate([one[24:], two[24:]], axis=0).astype(BF16)

    @pl.loop(0, 4)
    def _(n):
        rows = pl.ds(pl.multiple_of(192 * n, 192), 192)
        acc = lax.dot_general(right[rows, :], left[...], NT, preferred_element_type=F32)
        for b in range(8):
            for low in range(2):
                out_ref[16 * n + 2 * b + low] = acc[
                    24 * b : 24 * b + 24, LANES * low : LANES * (low + 1)
                ].astype(BF16)


def triangle(x):
    return pl.pallas_call(
        triangle_kernel,
        out_shape=jax.ShapeDtypeStruct((64, ROWS_PAD, LANES), BF16),
        in_specs=[pl.BlockSpec(memory_space=pltpu.VMEM)],
        out_specs=pl.BlockSpec(memory_space=pltpu.VMEM),
        scratch_shapes=[pltpu.VMEM((768, 768), BF16), pltpu.VMEM((768, 768), BF16)],
        compiler_params=pltpu.CompilerParams(vmem_limit_bytes=VMEM_LIMIT),
        name="triangle",
    )(x)


def finish_kernel(own_ref, sib_ref, g_ref, gate_weight_ref, gain_ref, weight_ref, out_ref, p32, gains, ws, mixed, packed):
    half = lax.axis_index("col") % 2

    @pl.loop(0, HALF)
    def _(c):
        for t in range(2):
            lanes = pl.ds(pl.multiple_of(128 * half + 128 * t, 128), 128)
            p32[t, pl.ds(pl.multiple_of(c * 24, 24), 24), :] = own_ref[c, :, lanes].astype(F32)
            p32[t, pl.ds(pl.multiple_of((HALF + c) * 24, 24), 24), :] = sib_ref[
                c, :, 128 * t : 128 * (t + 1)
            ].astype(F32)

    gains[...] = jnp.broadcast_to(gain_ref[...], (128, 128)).T
    ws[...] = weight_ref[...].astype(F32)
    first = pl.ds(pl.multiple_of(HALF * half, HALF), HALF)
    second = pl.ds(pl.multiple_of(HALF - HALF * half, HALF), HALF)
    gain = jnp.concatenate([gains[first, :], gains[second, :]], axis=0)
    gain = jnp.concatenate([gain, gain], axis=1)
    weight = jnp.concatenate([ws[first, :], ws[second, :]], axis=0).astype(BF16)

    @pl.loop(0, ROWS)
    def _(j):
        p = jnp.concatenate([p32[t, pl.ds(j, CHANNELS, stride=24), :] for t in range(2)], axis=1)
        center = p - jnp.mean(p, axis=0, keepdims=True)
        spread = jnp.mean(center * center, axis=0, keepdims=True)
        hidden = (center * lax.rsqrt(spread + 1e-05) * gain).astype(BF16)
        mixed[...] = lax.dot_general(hidden, weight, TN, preferred_element_type=F32)
        pairs = jnp.concatenate([g_ref[s, j].astype(F32) for s in range(8)], axis=0).astype(BF16)
        gate = sigmoid(jnp.dot(pairs, gate_weight_ref[...], preferred_element_type=F32))
        update = gate * mixed[pl.ds(pl.multiple_of(64 * half, 64), 192), :]
        for s in range(8):
            packed[22 * s : 22 * s + 24, :] = update[24 * s : 24 * s + 24]
        out_ref[j] = packed[0:COLS, :].astype(BF16)


def finish(own, sib, g, gate_weight, gain, weight):
    return pl.pallas_call(
        finish_kernel,
        out_shape=jax.ShapeDtypeStruct((ROWS, COLS, 128), BF16),
        in_specs=[pl.BlockSpec(memory_space=pltpu.VMEM)] * 6,
        out_specs=pl.BlockSpec(memory_space=pltpu.VMEM),
        scratch_shapes=[
            pltpu.VMEM((2, CHANNELS * 24, 128), F32),
            pltpu.VMEM((128, 128), F32),
            pltpu.VMEM((128, 128), F32),
            pltpu.VMEM((256, 128), F32),
            pltpu.VMEM((184, 128), F32),
        ],
        compiler_params=pltpu.CompilerParams(vmem_limit_bytes=VMEM_LIMIT),
        name="finish",
    )(own, sib, g, gate_weight, gain, weight)


def swap_kernel(src_ref, dst_ref, send, recv):
    row, col = place()
    barrier = pltpu.get_barrier_semaphore()

    def target(v):
        return 8 * col + v, row // 8

    def source(s):
        return 8 * col + s, row // 8

    for n in range(8):
        row2, col2 = target(n)

        @pl.when(jnp.logical_or(row2 != row, col2 != col))
        def _():
            pl.semaphore_signal(barrier, inc=1, device_id={"row": row2, "col": col2}, device_id_type=MESH)

    same = (row // 8 == col).astype(jnp.int32)
    pl.semaphore_wait(barrier, 8 - same)

    def copy(v):
        row2, col2 = target(v)
        return pltpu.make_async_remote_copy(
            src_ref=src_ref.at[v],
            dst_ref=dst_ref.at[row % 8],
            send_sem=send.at[v],
            recv_sem=recv.at[row % 8],
            device_id={"row": row2, "col": col2},
            device_id_type=MESH,
        )

    for v in range(8):
        row2, col2 = target(v)
        mine = jnp.logical_and(row2 == row, col2 == col)

        @pl.when(mine)
        def _():
            pltpu.make_async_copy(src_ref.at[v], dst_ref.at[v], recv.at[v]).start()

        @pl.when(jnp.logical_not(mine))
        def _():
            copy(v).start()

    for v in range(8):
        row2, col2 = target(v)
        mine = jnp.logical_and(row2 == row, col2 == col)

        @pl.when(jnp.logical_not(mine))
        def _():
            copy(v).wait_send()

        pltpu.make_async_copy(src_ref.at[v], dst_ref.at[v], recv.at[v]).wait()


def swap(x, collective_id):
    return pl.pallas_call(
        swap_kernel,
        out_shape=jax.ShapeDtypeStruct(x.shape, x.dtype),
        in_specs=[pl.BlockSpec(memory_space=pltpu.VMEM)],
        out_specs=pl.BlockSpec(memory_space=pltpu.VMEM),
        scratch_shapes=[pltpu.SemaphoreType.DMA((8,)), pltpu.SemaphoreType.DMA((8,))],
        compiler_params=pltpu.CompilerParams(
            collective_id=collective_id, has_side_effects=True, vmem_limit_bytes=VMEM_LIMIT
        ),
        name="swap",
    )(x)


def body(pair_map, in_gain, project_weight, gate_weight, out_gain, out_weight):
    half = lax.axis_index("col") % 2
    pairs = [(0, 1), (1, 0), (2, 3), (3, 2)]
    sibling = lax.ppermute(pair_map, "col", pairs)
    factors, normed = project(pair_map, sibling, in_gain.reshape(1, 128), project_weight)
    factors = exchange(factors, 0, "exchange_factors")
    normed = swap(normed.reshape(8, ROWS, ROWS_PAD, 128), 2)
    products = exchange(triangle(factors), 1, "exchange_products")
    theirs = lax.dynamic_slice_in_dim(products, 128 * (1 - half), 256, axis=2)
    theirs = lax.ppermute(theirs, "col", pairs)
    return finish(products, theirs, normed, gate_weight, out_gain.reshape(1, 128), out_weight)


def solution(mesh):
    return jax.shard_map(
        body,
        mesh=mesh,
        in_specs=(P("row", "col", None), P(), P(), P(), P(), P()),
        out_specs=P("row", "col", None),
        check_vma=False,
    )
```

time: 525 us -> 147 us (0.28)
  the two profiles are of different devices: /device:TPU:1 before, /device:TPU:24 now
where the time goes in v1:
time: 147 us; the launch traced here: 146 us
  Pallas kernels  140 us (95%)
  local copies, waits for them, and re-layouts  3.03 us (2%)
  waiting for transfers between devices  2.79 us (2%)
    pallas_call x2, Pallas kernels, exchange(): pl.pallas_call(exchange_kernel, out_shape=jax.ShapeDtypeStruct(x.shape, x...  67.1 us
    pallas_call x1, Pallas kernels, swap(): pl.pallas_call(swap_kernel, out_shape=jax.ShapeDtypeStruct(x.shape, x.dty...  39.3 us
    pallas_call x1, Pallas kernels, project(): pl.pallas_call(project_kernel, out_shape=(jax.ShapeDtypeStruct((HALF, 48,...  18.6 us
    pallas_call x1, Pallas kernels, finish(): pl.pallas_call(finish_kernel, out_shape=jax.ShapeDtypeStruct((ROWS, COLS,...  10.1 us
    pallas_call x1, Pallas kernels, triangle(): pl.pallas_call(triangle_kernel, out_shape=jax.ShapeDtypeStruct((64, ROWS_...  5.19 us
  transfers between devices with their start and end apart: 2, of which 1 were waited for; matrix products, arithmetic and copies ran while one was open for 0% of the time, Pallas kernels for 27%

profile of v1, /device:TPU:24, one launch (start us, length us, event | category | flops | bytes accessed | tf_op | source)
XLA Modules:
  0.0 146.2 jit_solution(7179031738797759153)
XLA Ops:
  0.0 0.0 collective-permute-start
  0.0 2.8 %collective-permute-done.sib_ref = bf16[22,176,128]{2,1,0:T(8,128)(2,1)S(1)} collective-permute-done((bf16[22,176,128]{2,1,0:T(8,128)(2,1)}, bf16[22,176,128]{2,1,0:T(8,128)(2,1)S(1)}, u32[]{:S(2)}, u32[]{:S(2)}) %collective-permute-start) | collective-permute-done | bytes 991264 | tf_op jit(solution)/shard_map/ppermute | solution.py:319
  2.8 0.0 copy-start
  2.8 0.9 copy-done
  3.7 18.6 %project.1 = (bf16[64,48,384]{2,1,0:T(8,128)(2,1)}, bf16[176,24,128]{2,1,0:T(8,128)(2,1)}) custom-call(bf16[22,176,128]{2,1,0:T(8,128)(2,1)} %own_ref.1, bf16[22,176,128]{2,1,0:T(8,128)(2,1)} %copy-done, f32[1,128]{1,0:T(1,128)} %bitcast.4, bf16[128,512]{1,0:T(8,128)(2,1)} %weight_ref.2), custom_call_target="tpu_custom_call" | custom-call | tf_op jit(solution)/shard_map/project/pallas_call | solution.py:88
  22.3 41.9 %exchange_factors.1.x_ref = bf16[64,48,384]{2,1,0:T(8,128)(2,1)} custom-call(bf16[64,48,384]{2,1,0:T(8,128)(2,1)} %get-tuple-element.7.src_ref), custom_call_target="tpu_custom_call" | custom-call | tf_op jit(solution)/shard_map/exchange_factors/pallas_call | solution.py:144
  64.2 5.2 %triangle.1.src_ref = bf16[64,24,384]{2,1,0:T(8,128)(2,1)} custom-call(bf16[64,48,384]{2,1,0:T(8,128)(2,1)} %exchange_factors.1.x_ref), custom_call_target="tpu_custom_call" | custom-call | tf_op jit(solution)/shard_map/triangle/pallas_call | solution.py:184
  69.4 25.2 %exchange_products.1.own_ref = bf16[64,24,384]{2,1,0:T(8,128)(2,1)} custom-call(bf16[64,24,384]{2,1,0:T(8,128)(2,1)} %triangle.1.src_ref), custom_call_target="tpu_custom_call" | custom-call | tf_op jit(solution)/shard_map/exchange_products/pallas_call | solution.py:144
  94.6 1.2 constant_dynamic-slice_fusion
  95.8 0.1 collective-permute-start.1
  95.9 39.3 %swap.1.g_ref = bf16[8,22,24,128]{3,2,1,0:T(8,128)(2,1)} custom-call(bf16[8,22,24,128]{3,2,1,0:T(8,128)(2,1)} %bitcast.3), custom_call_target="tpu_custom_call" | custom-call | tf_op jit(solution)/shard_map/swap/pallas_call | solution.py:303
  135.2 0.0 collective-permute-done.1.sib_ref
  135.2 0.0 copy-start.1
  135.2 0.9 copy-done.1
  136.1 10.1 %finish.1 = bf16[22,176,128]{2,1,0:T(8,128)(2,1)} custom-call(bf16[64,24,384]{2,1,0:T(8,128)(2,1)} %exchange_products.1.own_ref, bf16[64,24,256]{2,1,0:T(8,128)(2,1)} %copy-done.1, bf16[8,22,24,128]{3,2,1,0:T(8,128)(2,1)} %swap.1.g_ref, bf16[128,128]{1,0:T(8,128)(2,1)} %gate_weight_ref.1, f32[1,128]{1,0:T(1,128)} %bitcast.5, bf16[128,128]{1,0:T(8,128)(2,1)} %weight_ref.3), custom_call_target="tpu_custom_call" | custom-call | tf_op jit(solution)/shard_map/finish/pallas_call | solution.py:231
Async XLA Ops:
  0.0 2.8 %collective-permute-start = (bf16[22,176,128]{2,1,0:T(8,128)(2,1)}, bf16[22,176,128]{2,1,0:T(8,128)(2,1)S(1)}, u32[]{:S(2)}, u32[]{:S(2)}) collective-permute-start(bf16[22,176,128]{2,1,0:T(8,128)(2,1)} %own_ref.1), channel_id=1, source_target_pairs={{0,1},{1,0},{2,3},{3,2},{4,5},{5,4},{6,7},{7,6},{8,9},{9,8},{10,11... | collective-permute-start | bytes 2973704 | tf_op jit(solution)/shard_map/ppermute | solution.py:319
  2.8 0.9 copy-start
  95.8 39.4 %collective-permute-start.1 = (bf16[64,24,256]{2,1,0:T(8,128)(2,1)S(1)}, bf16[64,24,256]{2,1,0:T(8,128)(2,1)S(1)}, u32[]{:S(2)}, u32[]{:S(2)}) collective-permute-start(bf16[64,24,256]{2,1,0:T(8,128)(2,1)S(1)} %constant_dynamic-slice_fusion), channel_id=1, source_target_pairs={{0,1},{1,0},{2,3},{3,2},{4,5},{5,4},{6,7},{7,6},{8,9},{9,8},{10,11... | collective-permute-start | bytes 2359304 | tf_op jit(solution)/shard_map/ppermute | solution.py:325
  135.2 0.9 copy-start.1

commit v2 on v0

v2 whole, which is shorter than its diff:
```python
import functools

import jax
import jax.numpy as jnp
from jax import lax
from jax.experimental import pallas as pl
from jax.experimental.pallas import tpu as pltpu
from jax.sharding import PartitionSpec as P

MESH = pl.DeviceIdType.MESH
F32 = jnp.float32
BF16 = jnp.bfloat16
VMEM_LIMIT = 56 * 2**20

ROWS = 22
ROWS_PAD = 24
COLS = 176
CHANNELS = 128
HALF = 64
LANES = 384
BLOCKS = 32
NT = (((1,), (1,)), ((), ()))
TN = (((0,), (0,)), ((), ()))


def sigmoid(x):
    return 0.5 * jnp.tanh(0.5 * x) + 0.5


def place():
    row = lax.axis_index("row")
    col = lax.axis_index("col")
    return row, col


def chip_at(row, col, hop):
    z, y, x = row // 8, ((row // 4) % 2) * 2 + col // 2, row % 4
    z, y, x = (z + hop[0]) % 4, (y + hop[1]) % 4, (x + hop[2]) % 4
    row2 = z * 8 + (y // 2) * 4 + x
    low = y % 2
    return {"row": row2, "col": low * 2 + col % 2}, row2 * 2 + low


def hop_order():
    left = [(a, b, c) for a in range(4) for b in range(4) for c in range(4)][1:]
    use = [0] * 6
    order = []

    def after(hop):
        then = list(use)
        for axis, step in enumerate(hop):
            then[2 * axis] += (0, 2, 2, 0)[step]
            then[2 * axis + 1] += (0, 0, 2, 2)[step]
        return then

    def score(hop):
        then = after(hop)
        return max(then) - min(then), sum(v * v for v in then), (hop[0] * 37 + hop[1] * 11 + hop[2] * 5) % 17

    while left:
        best = min(left, key=score)
        use = after(best)
        left.remove(best)
        order.append(best)
    return order


HOPS = hop_order()
GROUPS = ((0, 8), (8, 16), (16, 22))


def wait_bytes(ref, sem):
    pltpu.make_async_copy(ref, ref, sem).wait()


def kernel(
    own_ref, sib_ref, gain_ref, weight_ref, gate_weight_ref, out_gain_ref, out_weight_ref, out_ref,
    wt, normed, lr32, g32, lr, g, lr_in, g_in, left, right, p, p_in, p_sib, p32, gates, gains, ws, mixed, packed,
    lr_send, lr_recv, g_send, g_recv, p_send, p_recv, sib_send, sib_recv,
):
    row, col = place()
    half = col % 2
    me = row * 2 + col // 2
    sibling = {"row": row, "col": col + 1 - 2 * half}
    barrier = pltpu.get_barrier_semaphore()

    def signal(device):
        pl.semaphore_signal(barrier, inc=1, device_id=device, device_id_type=MESH)

    signal(sibling)
    for hop in HOPS:
        signal(chip_at(row, col, hop)[0])
    partners = []
    for v in range(8):
        row2, col2 = 8 * col + v, row // 8
        mine = jnp.logical_and(row2 == row, col2 == col)
        partners.append(({"row": row2, "col": col2}, mine))

        @pl.when(jnp.logical_not(mine))
        def _():
            signal(partners[v][0])

    wt[...] = weight_ref[...].astype(F32).T
    parts = [wt[pl.ds(pl.multiple_of(128 * n + HALF * half, HALF), HALF), :] for n in range(4)]
    weight = jnp.concatenate(parts, axis=0).astype(BF16)
    ones = jnp.full((128, 128), 1.0 / 128, BF16)
    for u in range(11):
        normed[u, 2 * COLS :, :] = jnp.zeros((LANES - 2 * COLS, 128), BF16)
    for pad in (22, 23, 46, 47):
        for t in range(3):
            lr32[t, pl.ds(pad, HALF, stride=48), :] = jnp.zeros((HALF, 128), F32)
    for pad in (22, 23):
        g32[pl.ds(pad, COLS, stride=ROWS_PAD), :] = jnp.zeros((COLS, 128), F32)

    @pl.loop(0, 2)
    def _(n):
        for u in range(11):
            i = 11 * n + u
            x = jnp.concatenate([own_ref[i], sib_ref[i]], axis=0)
            center = x.astype(F32) - jnp.dot(x, ones, preferred_element_type=F32)
            spread = jnp.dot((center * center).astype(BF16), ones, preferred_element_type=F32)
            y = center * lax.rsqrt(spread + 1e-05) * gain_ref[...]
            normed[u, 0 : 2 * COLS, :] = y.astype(BF16)
            g32[pl.ds(i, COLS, stride=ROWS_PAD), :] = y[0:COLS]
        for u in range(11):
            i = 11 * n + u
            projected = lax.dot_general(weight, normed[u], NT, preferred_element_type=F32)
            one = sigmoid(projected[0:64]) * projected[64:128]
            two = sigmoid(projected[128:192]) * projected[192:256]
            for t in range(3):
                tile = slice(128 * t, 128 * (t + 1))
                lr32[t, pl.ds(i, HALF, stride=48), :] = one[:, tile]
                lr32[t, pl.ds(24 + i, HALF, stride=48), :] = two[:, tile]

    pl.semaphore_wait(barrier, 72 - (row // 8 == col).astype(jnp.int32))

    def pack_factors(chip):
        rows = pl.ds(pl.multiple_of(chip * 48, 48), 48)
        for t in range(3):
            lr[chip, :, 128 * t : 128 * (t + 1)] = lr32[t, rows, :].astype(BF16)

    for hop in HOPS:
        device, chip = chip_at(row, col, hop)
        pack_factors(chip)
        pltpu.make_async_remote_copy(
            src_ref=lr.at[chip],
            dst_ref=lr_in.at[me],
            send_sem=lr_send,
            recv_sem=lr_recv.at[row // 2],
            device_id=device,
            device_id_type=MESH,
        ).start()
    pack_factors(me)
    pltpu.make_async_copy(lr.at[me], lr_in.at[me], lr_recv.at[row // 2]).start()

    for v in range(8):
        device, mine = partners[v]

        @pl.loop(0, 2)
        def _(n):
            first = 22 * v + 11 * n
            rows = pl.ds(pl.multiple_of(first * ROWS_PAD, 8), 11 * ROWS_PAD)
            g[v, pl.ds(11 * n, 11)] = g32[rows, :].reshape(11, ROWS_PAD, 128).astype(BF16)

        @pl.when(mine)
        def _():
            pltpu.make_async_copy(g.at[v], g_in.at[v], g_recv.at[v]).start()

        @pl.when(jnp.logical_not(mine))
        def _():
            pltpu.make_async_remote_copy(
                src_ref=g.at[v],
                dst_ref=g_in.at[row % 8],
                send_sem=g_send.at[v],
                recv_sem=g_recv.at[row % 8],
                device_id=device,
                device_id_type=MESH,
            ).start()

    @pl.loop(0, BLOCKS // 2)
    def _(n):
        b = (row // 2 + n) % 16
        wait_bytes(lr_in.at[pl.ds(pl.multiple_of(4 * b, 4), 4)], lr_recv.at[b])
        for low in range(2):
            one = lr_in[4 * b + low].astype(F32)
            two = lr_in[4 * b + 2 + low].astype(F32)
            rows = pl.ds(pl.multiple_of(48 * b, 48), 48)
            lanes = slice(LANES * low, LANES * (low + 1))
            left[rows, lanes] = jnp.concatenate([one[:24], two[:24]], axis=0).astype(BF16)
            right[rows, lanes] = jnp.concatenate([one[24:], two[24:]], axis=0).astype(BF16)

    for n in range(2):
        acc = lax.dot_general(right[384 * n : 384 * (n + 1), :], left[...], NT, preferred_element_type=F32)
        for b in range(16):
            for low in range(2):
                for k in range(3):
                    p[k, 32 * n + 2 * b + low] = acc[
                        24 * b + 8 * k : 24 * b + 8 * k + 8, LANES * low : LANES * (low + 1)
                    ].astype(BF16)

    for k in range(3):
        pltpu.make_async_copy(p.at[k, me], p_in.at[k, me], p_recv.at[k]).start()
        for hop in HOPS:
            device, chip = chip_at(row, col, hop)
            pltpu.make_async_remote_copy(
                src_ref=p.at[k, chip],
                dst_ref=p_in.at[k, me],
                send_sem=p_send.at[k],
                recv_sem=p_recv.at[k],
                device_id=device,
                device_id_type=MESH,
            ).start()

    for s in range(8):
        wait_bytes(g_in.at[s], g_recv.at[s])

    @pl.loop(0, 2)
    def _(n):
        for u in range(11):
            j = 11 * n + u
            pairs = jnp.concatenate([g_in[s, j].astype(F32) for s in range(8)], axis=0).astype(BF16)
            gates[j] = sigmoid(jnp.dot(pairs, gate_weight_ref[...], preferred_element_type=F32))

    gains[...] = jnp.broadcast_to(out_gain_ref[...], (128, 128)).T
    ws[...] = out_weight_ref[...].astype(F32)
    first = pl.ds(pl.multiple_of(HALF * half, HALF), HALF)
    second = pl.ds(pl.multiple_of(HALF - HALF * half, HALF), HALF)
    gain = jnp.concatenate([gains[first, :], gains[second, :]], axis=0)
    gain = jnp.concatenate([gain, gain], axis=1)
    out_weight = jnp.concatenate([ws[first, :], ws[second, :]], axis=0).astype(BF16)

    for k, (start, stop) in enumerate(GROUPS):
        wait_bytes(p_in.at[k], p_recv.at[k])
        swap = pltpu.make_async_remote_copy(
            src_ref=p_in.at[k, :, :, pl.ds(pl.multiple_of(128 - 128 * half, 128), 256)],
            dst_ref=p_sib.at[k],
            send_sem=sib_send.at[k],
            recv_sem=sib_recv.at[k],
            device_id=sibling,
            device_id_type=MESH,
        )
        swap.start()
        for t in range(2):
            lanes = pl.ds(pl.multiple_of(128 * half + 128 * t, 128), 128)
            p32[t, 0:512, :] = p_in[k, :, :, lanes].astype(F32).reshape(512, 128)
        swap.wait()
        for t in range(2):
            p32[t, 512:1024, :] = p_sib[k, :, :, 128 * t : 128 * (t + 1)].astype(F32).reshape(512, 128)
        for j in range(start, stop):
            u = j - start
            q = jnp.concatenate([p32[t, pl.ds(u, CHANNELS, stride=8), :] for t in range(2)], axis=1)
            center = q - jnp.mean(q, axis=0, keepdims=True)
            spread = jnp.mean(center * center, axis=0, keepdims=True)
            hidden = (center * lax.rsqrt(spread + 1e-05) * gain).astype(BF16)
            mixed[u] = lax.dot_general(hidden, out_weight, TN, preferred_element_type=F32)
            update = gates[j] * mixed[u, pl.ds(pl.multiple_of(64 * half, 64), 192), :]
            for s in range(8):
                packed[u, 22 * s : 22 * s + 24, :] = update[24 * s : 24 * s + 24]
            out_ref[j] = packed[u, 0:COLS, :].astype(BF16)

    wait_bytes(lr.at[pl.ds(0, 63)], lr_send)
    for k in range(3):
        wait_bytes(p.at[k, pl.ds(0, 63)], p_send.at[k])
    for v in range(8):
        @pl.when(jnp.logical_not(partners[v][1]))
        def _():
            wait_bytes(g.at[v], g_send.at[v])


def fused(*args):
    vmem = pl.BlockSpec(memory_space=pltpu.VMEM)
    return pl.pallas_call(
        kernel,
        out_shape=jax.ShapeDtypeStruct((ROWS, COLS, 128), BF16),
        in_specs=[vmem] * 7,
        out_specs=vmem,
        scratch_shapes=[
            pltpu.VMEM((512, 128), F32),
            pltpu.VMEM((11, LANES, 128), BF16),
            pltpu.VMEM((3, HALF * 48, 128), F32),
            pltpu.VMEM((COLS * ROWS_PAD, 128), F32),
            pltpu.VMEM((64, 48, LANES), BF16),
            pltpu.VMEM((8, ROWS, ROWS_PAD, 128), BF16),
            pltpu.VMEM((64, 48, LANES), BF16),
            pltpu.VMEM((8, ROWS, ROWS_PAD, 128), BF16),
            pltpu.VMEM((768, 768), BF16),
            pltpu.VMEM((768, 768), BF16),
            pltpu.VMEM((3, 64, 8, LANES), BF16),
            pltpu.VMEM((3, 64, 8, LANES), BF16),
            pltpu.VMEM((3, 64, 8, 256), BF16),
            pltpu.VMEM((2, CHANNELS * 8, 128), F32),
            pltpu.VMEM((ROWS, 192, 128), F32),
            pltpu.VMEM((128, 128), F32),
            pltpu.VMEM((128, 128), F32),
            pltpu.VMEM((8, 256, 128), F32),
            pltpu.VMEM((8, 184, 128), F32),
            pltpu.SemaphoreType.DMA,
            pltpu.SemaphoreType.DMA((16,)),
            pltpu.SemaphoreType.DMA((8,)),
            pltpu.SemaphoreType.DMA((8,)),
            pltpu.SemaphoreType.DMA((3,)),
            pltpu.SemaphoreType.DMA((3,)),
            pltpu.SemaphoreType.DMA((3,)),
            pltpu.SemaphoreType.DMA((3,)),
        ],
        compiler_params=pltpu.CompilerParams(
            collective_id=0, has_side_effects=True, vmem_limit_bytes=VMEM_LIMIT
        ),
        name="triangle_update",
    )(*args)


def body(pair_map, in_gain, project_weight, gate_weight, out_gain, out_weight):
    sibling = lax.ppermute(pair_map, "col", [(0, 1), (1, 0), (2, 3), (3, 2)])
    return fused(
        pair_map, sibling, in_gain.reshape(1, 128), project_weight, gate_weight, out_gain.reshape(1, 128), out_weight
    )


def solution(mesh):
    return jax.shard_map(
        body,
        mesh=mesh,
        in_specs=(P("row", "col", None), P(), P(), P(), P(), P()),
        out_specs=P("row", "col", None),
        check_vma=False,
    )
```

time: 525 us -> 98.2 us (0.19)
  the two profiles are of different devices: /device:TPU:1 before, /device:TPU:3 now
where the time goes in v2:
time: 98.2 us; the launch traced here: 98 us
  Pallas kernels  91.8 us (93%)
  local copies, waits for them, and re-layouts  3.16 us (3%)
  waiting for transfers between devices  2.42 us (2%)
    pallas_call x1, Pallas kernels, fused(): pl.pallas_call(kernel, out_shape=jax.ShapeDtypeStruct((ROWS, COLS, 128),...  91.8 us
    unnamed x3, local copies, waits for them, and re-layouts  3.16 us
    ppermute x1, waiting for transfers between devices, body(): sibling = lax.ppermute(pair_map, 'col', [(0, 1), (1, 0), (2, 3), (3, 2)])  2.42 us
  transfers between devices with their start and end apart: 1, of which 1 were waited for; matrix products, arithmetic and copies ran while one was open for 0% of the time, Pallas kernels for 0%

profile of v2, /device:TPU:3, one launch (start us, length us, event | category | flops | bytes accessed | tf_op | source)
XLA Modules:
  0.0 98.0 jit_solution(17227606799973432959)
XLA Ops:
  0.0 0.7 collective-permute-start
  0.7 2.4 %collective-permute-done.sib_ref = bf16[22,176,128]{2,1,0:T(8,128)(2,1)S(1)} collective-permute-done((bf16[22,176,128]{2,1,0:T(8,128)(2,1)}, bf16[22,176,128]{2,1,0:T(8,128)(2,1)S(1)}, u32[]{:S(2)}, u32[]{:S(2)}) %collective-permute-start) | collective-permute-done | bytes 991264 | tf_op jit(solution)/shard_map/ppermute | solution.py:314
  3.1 0.0 copy-start
  3.1 0.9 copy-done
  4.0 91.8 %triangle_update.1 = bf16[22,176,128]{2,1,0:T(8,128)(2,1)} custom-call(bf16[22,176,128]{2,1,0:T(8,128)(2,1)} %own_ref.1, bf16[22,176,128]{2,1,0:T(8,128)(2,1)} %copy-done, f32[1,128]{1,0:T(1,128)} %bitcast.2, bf16[128,512]{1,0:T(8,128)(2,1)} %weight_ref.1, bf16[128,128]{1,0:T(8,128)(2,1)} %gate_weight_ref.1, f32[1,128]{1,0:T(1,128)} %bitcast.3, ...), custom_call_target="tpu_custom_call" | custom-call | tf_op jit(solution)/shard_map/triangle_update/pallas_call | solution.py:272
  95.8 2.2 %copy.8 = bf16[22,176,128]{2,1,0:T(8,128)(2,1)} copy(bf16[22,176,128]{2,1,0:T(8,128)(2,1)} %triangle_update.1) | data formatting | bytes 1982464
Async XLA Ops:
  0.0 3.1 %collective-permute-start = (bf16[22,176,128]{2,1,0:T(8,128)(2,1)}, bf16[22,176,128]{2,1,0:T(8,128)(2,1)S(1)}, u32[]{:S(2)}, u32[]{:S(2)}) collective-permute-start(bf16[22,176,128]{2,1,0:T(8,128)(2,1)} %own_ref.1), channel_id=1, source_target_pairs={{0,1},{1,0},{2,3},{3,2},{4,5},{5,4},{6,7},{7,6},{8,9},{9,8},{10,11... | collective-permute-start | bytes 2973704 | tf_op jit(solution)/shard_map/ppermute | solution.py:314
  3.1 0.9 copy-start

commit v3 on v2

--- a/solution.py
+++ b/solution.py
@@ -75,8 +75,8 @@
 
 def kernel(
     own_ref, sib_ref, gain_ref, weight_ref, gate_weight_ref, out_gain_ref, out_weight_ref, out_ref,
-    wt, normed, lr32, g32, lr, g, lr_in, g_in, left, right, p, p_in, p_sib, p32, gates, gains, ws, mixed, packed,
-    lr_send, lr_recv, g_send, g_recv, p_send, p_recv, sib_send, sib_recv,
+    own, wt, normed, lr32, g32, lr, g, g_relay, lr_in, g_in, left, right, p, p_in, p_sib, p32, gates, gains, ws, mixed, packed,
+    own_sem, lr_send, lr_recv, g_send, g_recv, relay_send, relay_recv, p_send, p_recv, sib_send, sib_recv,
 ):
     row, col = place()
     half = col % 2
@@ -87,52 +87,85 @@
     def signal(device):
         pl.semaphore_signal(barrier, inc=1, device_id=device, device_id_type=MESH)
 
+    z, y_hi, x = row // 8, (row // 4) % 2, row % 4
+    base = 8 * col + 4 * y_hi
+    other = (z + 2) % 4
+    owners, relays = [], []
+    for n in range(4):
+        x2 = (x + n) % 4
+        owners.append((4 * y_hi + x2, {"row": base + x2, "col": z}))
+        relays.append((4 - 4 * y_hi + x2, {"row": base + x2, "col": other}))
+    forward = {"row": row + 4 - 8 * y_hi, "col": (col + 2) % 4}
+    is_own = z == col
+
     signal(sibling)
     for hop in HOPS:
         signal(chip_at(row, col, hop)[0])
-    partners = []
-    for v in range(8):
-        row2, col2 = 8 * col + v, row // 8
-        mine = jnp.logical_and(row2 == row, col2 == col)
-        partners.append(({"row": row2, "col": col2}, mine))
-
-        @pl.when(jnp.logical_not(mine))
+    for n in range(4):
+        signal({"row": 8 * ((col + 2) % 4) + 4 * y_hi + n, "col": z})
+
+        @pl.when(jnp.logical_or(jnp.logical_not(is_own), n != x))
         def _():
-            signal(partners[v][0])
+            signal({"row": base + n, "col": z})
+
+    own_copy = pltpu.make_async_copy(own_ref, own, own_sem)
+    own_copy.start()
 
     wt[...] = weight_ref[...].astype(F32).T
     parts = [wt[pl.ds(pl.multiple_of(128 * n + HALF * half, HALF), HALF), :] for n in range(4)]
     weight = jnp.concatenate(parts, axis=0).astype(BF16)
     ones = jnp.full((128, 128), 1.0 / 128, BF16)
-    for u in range(11):
-        normed[u, 2 * COLS :, :] = jnp.zeros((LANES - 2 * COLS, 128), BF16)
+    for i in range(ROWS):
+        normed[i, 2 * COLS :, :] = jnp.zeros((LANES - 2 * COLS, 128), BF16)
     for pad in (22, 23, 46, 47):
         for t in range(3):
             lr32[t, pl.ds(pad, HALF, stride=48), :] = jnp.zeros((HALF, 128), F32)
     for pad in (22, 23):
         g32[pl.ds(pad, COLS, stride=ROWS_PAD), :] = jnp.zeros((COLS, 128), F32)
+    own_copy.wait()
 
     @pl.loop(0, 2)
     def _(n):
         for u in range(11):
             i = 11 * n + u
-            x = jnp.concatenate([own_ref[i], sib_ref[i]], axis=0)
-            center = x.astype(F32) - jnp.dot(x, ones, preferred_element_type=F32)
+            v = jnp.concatenate([own[i], sib_ref[i]], axis=0)
+            center = v.astype(F32) - jnp.dot(v, ones, preferred_element_type=F32)
             spread = jnp.dot((center * center).astype(BF16), ones, preferred_element_type=F32)
             y = center * lax.rsqrt(spread + 1e-05) * gain_ref[...]
-            normed[u, 0 : 2 * COLS, :] = y.astype(BF16)
+            normed[i, 0 : 2 * COLS, :] = y.astype(BF16)
             g32[pl.ds(i, COLS, stride=ROWS_PAD), :] = y[0:COLS]
+
+    def pack_pairs(v):
+        for n in range(2):
+            rows = pl.ds(pl.multiple_of((22 * v + 11 * n) * ROWS_PAD, 8), 11 * ROWS_PAD)
+            g[v, pl.ds(11 * n, 11)] = g32[rows, :].reshape(11, ROWS_PAD, 128).astype(BF16)
+
+    for v, _ in relays:
+        pack_pairs(v)
+
+    pl.semaphore_wait(barrier, 72 - is_own.astype(jnp.int32))
+
+    for v, device in relays:
+        pltpu.make_async_remote_copy(
+            src_ref=g.at[v],
+            dst_ref=g_relay.at[x],
+            send_sem=g_send.at[v],
+            recv_sem=relay_recv.at[x],
+            device_id=device,
+            device_id_type=MESH,
+        ).start()
+
+    @pl.loop(0, 2)
+    def _(n):
         for u in range(11):
             i = 11 * n + u
-            projected = lax.dot_general(weight, normed[u], NT, preferred_element_type=F32)
+            projected = lax.dot_general(weight, normed[i], NT, preferred_element_type=F32)
             one = sigmoid(projected[0:64]) * projected[64:128]
             two = sigmoid(projected[128:192]) * projected[192:256]
             for t in range(3):
                 tile = slice(128 * t, 128 * (t + 1))
                 lr32[t, pl.ds(i, HALF, stride=48), :] = one[:, tile]
                 lr32[t, pl.ds(24 + i, HALF, stride=48), :] = two[:, tile]
-
-    pl.semaphore_wait(barrier, 72 - (row // 8 == col).astype(jnp.int32))
 
     def pack_factors(chip):
         rows = pl.ds(pl.multiple_of(chip * 48, 48), 48)
@@ -153,21 +186,10 @@
     pack_factors(me)
     pltpu.make_async_copy(lr.at[me], lr_in.at[me], lr_recv.at[row // 2]).start()
 
-    for v in range(8):
-        device, mine = partners[v]
-
-        @pl.loop(0, 2)
-        def _(n):
-            first = 22 * v + 11 * n
-            rows = pl.ds(pl.multiple_of(first * ROWS_PAD, 8), 11 * ROWS_PAD)
-            g[v, pl.ds(11 * n, 11)] = g32[rows, :].reshape(11, ROWS_PAD, 128).astype(BF16)
-
-        @pl.when(mine)
-        def _():
-            pltpu.make_async_copy(g.at[v], g_in.at[v], g_recv.at[v]).start()
-
-        @pl.when(jnp.logical_not(mine))
-        def _():
+    for n, (v, device) in enumerate(owners):
+        pack_pairs(v)
+
+        def send_pairs():
             pltpu.make_async_remote_copy(
                 src_ref=g.at[v],
                 dst_ref=g_in.at[row % 8],
@@ -176,6 +198,28 @@
                 device_id=device,
                 device_id_type=MESH,
             ).start()
+
+        if n == 0:
+
+            @pl.when(is_own)
+            def _():
+                pltpu.make_async_copy(g.at[v], g_in.at[v], g_recv.at[v]).start()
+
+            pl.when(jnp.logical_not(is_own))(send_pairs)
+        else:
+            send_pairs()
+
+    for n in range(4):
+        s = (x + 4 - n) % 4
+        wait_bytes(g_relay.at[s], relay_recv.at[s])
+        pltpu.make_async_remote_copy(
+            src_ref=g_relay.at[s],
+            dst_ref=g_in.at[4 * y_hi + s],
+            send_sem=relay_send.at[s],
+            recv_sem=g_recv.at[4 * y_hi + s],
+            device_id=forward,
+            device_id_type=MESH,
+        ).start()
 
     @pl.loop(0, BLOCKS // 2)
     def _(n):
@@ -261,10 +305,14 @@
     wait_bytes(lr.at[pl.ds(0, 63)], lr_send)
     for k in range(3):
         wait_bytes(p.at[k, pl.ds(0, 63)], p_send.at[k])
-    for v in range(8):
-        @pl.when(jnp.logical_not(partners[v][1]))
-        def _():
-            wait_bytes(g.at[v], g_send.at[v])
+    for v, _ in relays + owners[1:]:
+        wait_bytes(g.at[v], g_send.at[v])
+    for s in range(4):
+        wait_bytes(g_relay.at[s], relay_send.at[s])
+
+    @pl.when(jnp.logical_not(is_own))
+    def _():
+        wait_bytes(g.at[owners[0][0]], g_send.at[owners[0][0]])
 
 
 def fused(*args):
@@ -272,15 +320,17 @@
     return pl.pallas_call(
         kernel,
         out_shape=jax.ShapeDtypeStruct((ROWS, COLS, 128), BF16),
-        in_specs=[vmem] * 7,
+        in_specs=[pl.BlockSpec(memory_space=pl.ANY)] + [vmem] * 6,
         out_specs=vmem,
         scratch_shapes=[
+            pltpu.VMEM((ROWS, COLS, 128), BF16),
             pltpu.VMEM((512, 128), F32),
-            pltpu.VMEM((11, LANES, 128), BF16),
+            pltpu.VMEM((ROWS, LANES, 128), BF16),
             pltpu.VMEM((3, HALF * 48, 128), F32),
             pltpu.VMEM((COLS * ROWS_PAD, 128), F32),
             pltpu.VMEM((64, 48, LANES), BF16),
             pltpu.VMEM((8, ROWS, ROWS_PAD, 128), BF16),
+            pltpu.VMEM((4, ROWS, ROWS_PAD, 128), BF16),
             pltpu.VMEM((64, 48, LANES), BF16),
             pltpu.VMEM((8, ROWS, ROWS_PAD, 128), BF16),
             pltpu.VMEM((768, 768), BF16),
@@ -295,9 +345,12 @@
             pltpu.VMEM((8, 256, 128), F32),
             pltpu.VMEM((8, 184, 128), F32),
             pltpu.SemaphoreType.DMA,
+            pltpu.SemaphoreType.DMA,
             pltpu.SemaphoreType.DMA((16,)),
             pltpu.SemaphoreType.DMA((8,)),
             pltpu.SemaphoreType.DMA((8,)),
+            pltpu.SemaphoreType.DMA((4,)),
+            pltpu.SemaphoreType.DMA((4,)),
             pltpu.SemaphoreType.DMA((3,)),
             pltpu.SemaphoreType.DMA((3,)),
             pltpu.SemaphoreType.DMA((3,)),

time: 98.2 us -> 88 us (0.90)
  the two profiles are of different devices: /device:TPU:3 before, /device:TPU:1 now
where the time goes in v3:
time: 88 us; the launch traced here: 87.8 us
  Pallas kernels  80.8 us (92%)
  local copies, waits for them, and re-layouts  3.16 us (4%)
  waiting for transfers between devices  2.42 us (3%)
  starting transfers between devices  1.42 us (2%)
    pallas_call x1, Pallas kernels, fused(): pl.pallas_call(kernel, out_shape=jax.ShapeDtypeStruct((ROWS, COLS, 128),...  80.8 us
    unnamed x3, local copies, waits for them, and re-layouts  3.16 us
    ppermute x1, waiting for transfers between devices, body(): sibling = lax.ppermute(pair_map, 'col', [(0, 1), (1, 0), (2, 3), (3, 2)])  2.42 us
  transfers between devices with their start and end apart: 1, of which 1 were waited for; matrix products, arithmetic and copies ran while one was open for 0% of the time, Pallas kernels for 0%

profile of v3, /device:TPU:1, one launch (start us, length us, event | category | flops | bytes accessed | tf_op | source)
XLA Modules:
  0.0 87.8 jit_solution(9519846056001405446)
XLA Ops:
  0.0 1.4 %collective-permute-start = (bf16[22,176,128]{2,1,0:T(8,128)(2,1)}, bf16[22,176,128]{2,1,0:T(8,128)(2,1)S(1)}, u32[]{:S(2)}, u32[]{:S(2)}) collective-permute-start(bf16[22,176,128]{2,1,0:T(8,128)(2,1)} %own_ref.1), channel_id=1, source_target_pairs={{0,1},{1,0},{2,3},{3,2},{4,5},{5,4},{6,7},{7,6},{8,9},{9,8},{10,11... | collective-permute-start | bytes 2973704 | tf_op jit(solution)/shard_map/ppermute | solution.py:367
  1.4 2.4 %collective-permute-done.sib_ref = bf16[22,176,128]{2,1,0:T(8,128)(2,1)S(1)} collective-permute-done((bf16[22,176,128]{2,1,0:T(8,128)(2,1)}, bf16[22,176,128]{2,1,0:T(8,128)(2,1)S(1)}, u32[]{:S(2)}, u32[]{:S(2)}) %collective-permute-start) | collective-permute-done | bytes 991264 | tf_op jit(solution)/shard_map/ppermute | solution.py:367
  3.8 0.0 copy-start
  3.8 0.9 %copy-done = bf16[22,176,128]{2,1,0:T(8,128)(2,1)} copy-done((bf16[22,176,128]{2,1,0:T(8,128)(2,1)}, bf16[22,176,128]{2,1,0:T(8,128)(2,1)S(1)}, u32[]{:S(2)}) %copy-start) | copy-done | bytes 991256
  4.8 80.8 %triangle_update.1 = bf16[22,176,128]{2,1,0:T(8,128)(2,1)} custom-call(bf16[22,176,128]{2,1,0:T(8,128)(2,1)} %own_ref.1, bf16[22,176,128]{2,1,0:T(8,128)(2,1)} %copy-done, f32[1,128]{1,0:T(1,128)} %bitcast.2, bf16[128,512]{1,0:T(8,128)(2,1)} %weight_ref.1, bf16[128,128]{1,0:T(8,128)(2,1)} %gate_weight_ref.1, f32[1,128]{1,0:T(1,128)} %bitcast.3, ...), custom_call_target="tpu_custom_call" | custom-call | tf_op jit(solution)/shard_map/triangle_update/pallas_call | solution.py:320
  85.6 2.2 %copy.8 = bf16[22,176,128]{2,1,0:T(8,128)(2,1)} copy(bf16[22,176,128]{2,1,0:T(8,128)(2,1)} %triangle_update.1) | data formatting | bytes 1982464
Async XLA Ops:
  0.0 3.8 %collective-permute-start = (bf16[22,176,128]{2,1,0:T(8,128)(2,1)}, bf16[22,176,128]{2,1,0:T(8,128)(2,1)S(1)}, u32[]{:S(2)}, u32[]{:S(2)}) collective-permute-start(bf16[22,176,128]{2,1,0:T(8,128)(2,1)} %own_ref.1), channel_id=1, source_target_pairs={{0,1},{1,0},{2,3},{3,2},{4,5},{5,4},{6,7},{7,6},{8,9},{9,8},{10,11... | collective-permute-start | bytes 2973704 | tf_op jit(solution)/shard_map/ppermute | solution.py:367
  3.8 0.9 %copy-start = (bf16[22,176,128]{2,1,0:T(8,128)(2,1)}, bf16[22,176,128]{2,1,0:T(8,128)(2,1)S(1)}, u32[]{:S(2)}) copy-start(bf16[22,176,128]{2,1,0:T(8,128)(2,1)S(1)} %collective-permute-done.sib_ref) | copy-start | bytes 2973700

commit v4 on v3

--- a/solution.py
+++ b/solution.py
@@ -74,9 +74,9 @@
 
 
 def kernel(
-    own_ref, sib_ref, gain_ref, weight_ref, gate_weight_ref, out_gain_ref, out_weight_ref, out_ref,
-    own, wt, normed, lr32, g32, lr, g, g_relay, lr_in, g_in, left, right, p, p_in, p_sib, p32, gates, gains, ws, mixed, packed,
-    own_sem, lr_send, lr_recv, g_send, g_recv, relay_send, relay_recv, p_send, p_recv, sib_send, sib_recv,
+    own_ref, gain_ref, weight_ref, gate_weight_ref, out_gain_ref, out_weight_ref, out_ref,
+    own, sib, wt, first, rest, lr32, g32, lr, g, g_relay, lr_in, g_in, left, right, p, p_in, p_sib, p32, gates, gains, ws, mixed, packed, out,
+    own_sem, map_send, map_recv, lr_send, lr_recv, g_send, g_recv, relay_send, relay_recv, p_send, p_recv, sib_send, sib_recv, out_sem,
 ):
     row, col = place()
     half = col % 2
@@ -116,36 +116,65 @@
     weight = jnp.concatenate(parts, axis=0).astype(BF16)
     ones = jnp.full((128, 128), 1.0 / 128, BF16)
     for i in range(ROWS):
-        normed[i, 2 * COLS :, :] = jnp.zeros((LANES - 2 * COLS, 128), BF16)
+        rest[i, 224:256, :] = jnp.zeros((32, 128), BF16)
     for pad in (22, 23, 46, 47):
         for t in range(3):
             lr32[t, pl.ds(pad, HALF, stride=48), :] = jnp.zeros((HALF, 128), F32)
     for pad in (22, 23):
         g32[pl.ds(pad, COLS, stride=ROWS_PAD), :] = jnp.zeros((COLS, 128), F32)
+
+    def layer_norm(v):
+        center = v.astype(F32) - jnp.dot(v, ones, preferred_element_type=F32)
+        spread = jnp.dot((center * center).astype(BF16), ones, preferred_element_type=F32)
+        return center * lax.rsqrt(spread + 1e-05) * gain_ref[...]
+
+    def factors(i, t, projected):
+        one = sigmoid(projected[0:64]) * projected[64:128]
+        two = sigmoid(projected[128:192]) * projected[192:256]
+        lr32[t, pl.ds(i, HALF, stride=48), :] = one
+        lr32[t, pl.ds(24 + i, HALF, stride=48), :] = two
+
+    def pack_pairs(v):
+        for n in range(2):
+            rows = pl.ds(pl.multiple_of((22 * v + 11 * n) * ROWS_PAD, 8), 11 * ROWS_PAD)
+            g[v, pl.ds(11 * n, 11)] = g32[rows, :].reshape(11, ROWS_PAD, 128).astype(BF16)
+
     own_copy.wait()
 
     @pl.loop(0, 2)
     def _(n):
         for u in range(11):
             i = 11 * n + u
-            v = jnp.concatenate([own[i], sib_ref[i]], axis=0)
-            center = v.astype(F32) - jnp.dot(v, ones, preferred_element_type=F32)
-            spread = jnp.dot((center * center).astype(BF16), ones, preferred_element_type=F32)
-            y = center * lax.rsqrt(spread + 1e-05) * gain_ref[...]
-            normed[i, 0 : 2 * COLS, :] = y.astype(BF16)
-            g32[pl.ds(i, COLS, stride=ROWS_PAD), :] = y[0:COLS]
-
-    def pack_pairs(v):
-        for n in range(2):
-            rows = pl.ds(pl.multiple_of((22 * v + 11 * n) * ROWS_PAD, 8), 11 * ROWS_PAD)
-            g[v, pl.ds(11 * n, 11)] = g32[rows, :].reshape(11, ROWS_PAD, 128).astype(BF16)
-
-    for v, _ in relays:
-        pack_pairs(v)
+            y = layer_norm(own[i])
+            first[i] = y[0:128].astype(BF16)
+            rest[i, 128:176, :] = y[128:176].astype(BF16)
+            g32[pl.ds(i, COLS, stride=ROWS_PAD), :] = y
+
+    for n in (0, 2):
+        pack_pairs(relays[n][0])
+        pack_pairs(owners[n + 1][0])
+
+    for n in range(11):
+        pair = first[2 * n : 2 * n + 2].reshape(256, 128)
+        projected = lax.dot_general(weight, pair, NT, preferred_element_type=F32)
+        factors(2 * n, 0, projected[:, 0:128])
+        factors(2 * n + 1, 0, projected[:, 128:256])
 
     pl.semaphore_wait(barrier, 72 - is_own.astype(jnp.int32))
 
-    for v, device in relays:
+    def swap_maps(n):
+        rows = pl.ds(11 * n, 11)
+        return pltpu.make_async_remote_copy(
+            src_ref=own.at[rows],
+            dst_ref=sib.at[rows],
+            send_sem=map_send.at[n],
+            recv_sem=map_recv.at[n],
+            device_id=sibling,
+            device_id_type=MESH,
+        )
+
+    def send_relayed(n):
+        v, device = relays[n]
         pltpu.make_async_remote_copy(
             src_ref=g.at[v],
             dst_ref=g_relay.at[x],
@@ -155,17 +184,60 @@
             device_id_type=MESH,
         ).start()
 
-    @pl.loop(0, 2)
-    def _(n):
-        for u in range(11):
-            i = 11 * n + u
-            projected = lax.dot_general(weight, normed[i], NT, preferred_element_type=F32)
-            one = sigmoid(projected[0:64]) * projected[64:128]
-            two = sigmoid(projected[128:192]) * projected[192:256]
-            for t in range(3):
-                tile = slice(128 * t, 128 * (t + 1))
-                lr32[t, pl.ds(i, HALF, stride=48), :] = one[:, tile]
-                lr32[t, pl.ds(24 + i, HALF, stride=48), :] = two[:, tile]
+    def send_direct(n):
+        v, device = owners[n]
+
+        def send_pairs():
+            pltpu.make_async_remote_copy(
+                src_ref=g.at[v],
+                dst_ref=g_in.at[row % 8],
+                send_sem=g_send.at[v],
+                recv_sem=g_recv.at[row % 8],
+                device_id=device,
+                device_id_type=MESH,
+            ).start()
+
+        if n == 0:
+
+            @pl.when(is_own)
+            def _():
+                pltpu.make_async_copy(g.at[v], g_in.at[v], g_recv.at[v]).start()
+
+            pl.when(jnp.logical_not(is_own))(send_pairs)
+        else:
+            send_pairs()
+
+    def send_on(n):
+        s = (x + 4 - n) % 4
+        wait_bytes(g_relay.at[s], relay_recv.at[s])
+        pltpu.make_async_remote_copy(
+            src_ref=g_relay.at[s],
+            dst_ref=g_in.at[4 * y_hi + s],
+            send_sem=relay_send.at[s],
+            recv_sem=g_recv.at[4 * y_hi + s],
+            device_id=forward,
+            device_id_type=MESH,
+        ).start()
+
+    for n in range(2):
+        swap_maps(n).start()
+    for n in (0, 2):
+        send_relayed(n)
+        send_direct(n + 1)
+    for n in (0, 2):
+        pack_pairs(relays[n + 1][0])
+        pack_pairs(owners[n][0])
+
+    for n in range(2):
+        swap_maps(n).wait()
+        for i in range(11 * n, 11 * n + 11):
+            y = layer_norm(sib[i]).astype(BF16)
+            rest[i, 0:128, :] = y[0:128]
+            rest[i, 176:224, :] = y[128:176]
+        for i in range(11 * n, 11 * n + 11):
+            projected = lax.dot_general(weight, rest[i], NT, preferred_element_type=F32)
+            factors(i, 1, projected[:, 0:128])
+            factors(i, 2, projected[:, 128:256])
 
     def pack_factors(chip):
         rows = pl.ds(pl.multiple_of(chip * 48, 48), 48)
@@ -186,40 +258,11 @@
     pack_factors(me)
     pltpu.make_async_copy(lr.at[me], lr_in.at[me], lr_recv.at[row // 2]).start()
 
-    for n, (v, device) in enumerate(owners):
-        pack_pairs(v)
-
-        def send_pairs():
-            pltpu.make_async_remote_copy(
-                src_ref=g.at[v],
-                dst_ref=g_in.at[row % 8],
-                send_sem=g_send.at[v],
-                recv_sem=g_recv.at[row % 8],
-                device_id=device,
-                device_id_type=MESH,
-            ).start()
-
-        if n == 0:
-
-            @pl.when(is_own)
-            def _():
-                pltpu.make_async_copy(g.at[v], g_in.at[v], g_recv.at[v]).start()
-
-            pl.when(jnp.logical_not(is_own))(send_pairs)
-        else:
-            send_pairs()
-
-    for n in range(4):
-        s = (x + 4 - n) % 4
-        wait_bytes(g_relay.at[s], relay_recv.at[s])
-        pltpu.make_async_remote_copy(
-            src_ref=g_relay.at[s],
-            dst_ref=g_in.at[4 * y_hi + s],
-            send_sem=relay_send.at[s],
-            recv_sem=g_recv.at[4 * y_hi + s],
-            device_id=forward,
-            device_id_type=MESH,
-        ).start()
+    for n in (0, 2):
+        send_relayed(n + 1)
+        send_direct(n)
+    for n in (0, 2):
+        send_on(n)
 
     @pl.loop(0, BLOCKS // 2)
     def _(n):
@@ -242,6 +285,8 @@
                         24 * b + 8 * k : 24 * b + 8 * k + 8, LANES * low : LANES * (low + 1)
                     ].astype(BF16)
 
+    for n in (1, 3):
+        send_on(n)
     for k in range(3):
         pltpu.make_async_copy(p.at[k, me], p_in.at[k, me], p_recv.at[k]).start()
         for hop in HOPS:
@@ -267,11 +312,11 @@
 
     gains[...] = jnp.broadcast_to(out_gain_ref[...], (128, 128)).T
     ws[...] = out_weight_ref[...].astype(F32)
-    first = pl.ds(pl.multiple_of(HALF * half, HALF), HALF)
-    second = pl.ds(pl.multiple_of(HALF - HALF * half, HALF), HALF)
-    gain = jnp.concatenate([gains[first, :], gains[second, :]], axis=0)
+    ours = pl.ds(pl.multiple_of(HALF * half, HALF), HALF)
+    theirs = pl.ds(pl.multiple_of(HALF - HALF * half, HALF), HALF)
+    gain = jnp.concatenate([gains[ours, :], gains[theirs, :]], axis=0)
     gain = jnp.concatenate([gain, gain], axis=1)
-    out_weight = jnp.concatenate([ws[first, :], ws[second, :]], axis=0).astype(BF16)
+    out_weight = jnp.concatenate([ws[ours, :], ws[theirs, :]], axis=0).astype(BF16)
 
     for k, (start, stop) in enumerate(GROUPS):
         wait_bytes(p_in.at[k], p_recv.at[k])
@@ -300,8 +345,13 @@
             update = gates[j] * mixed[u, pl.ds(pl.multiple_of(64 * half, 64), 192), :]
             for s in range(8):
                 packed[u, 22 * s : 22 * s + 24, :] = update[24 * s : 24 * s + 24]
-            out_ref[j] = packed[u, 0:COLS, :].astype(BF16)
-
+            out[j] = packed[u, 0:COLS, :].astype(BF16)
+        group = pl.ds(start, stop - start)
+        pltpu.make_async_copy(out.at[group], out_ref.at[group], out_sem.at[k]).start()
+
+    for k, (start, stop) in enumerate(GROUPS):
+        group = pl.ds(start, stop - start)
+        pltpu.make_async_copy(out.at[group], out_ref.at[group], out_sem.at[k]).wait()
     wait_bytes(lr.at[pl.ds(0, 63)], lr_send)
     for k in range(3):
         wait_bytes(p.at[k, pl.ds(0, 63)], p_send.at[k])
@@ -320,12 +370,14 @@
     return pl.pallas_call(
         kernel,
         out_shape=jax.ShapeDtypeStruct((ROWS, COLS, 128), BF16),
-        in_specs=[pl.BlockSpec(memory_space=pl.ANY)] + [vmem] * 6,
-        out_specs=vmem,
+        in_specs=[pl.BlockSpec(memory_space=pl.ANY)] + [vmem] * 5,
+        out_specs=pl.BlockSpec(memory_space=pl.ANY),
         scratch_shapes=[
             pltpu.VMEM((ROWS, COLS, 128), BF16),
+            pltpu.VMEM((ROWS, COLS, 128), BF16),
             pltpu.VMEM((512, 128), F32),
-            pltpu.VMEM((ROWS, LANES, 128), BF16),
+            pltpu.VMEM((ROWS, 128, 128), BF16),
+            pltpu.VMEM((ROWS, 256, 128), BF16),
             pltpu.VMEM((3, HALF * 48, 128), F32),
             pltpu.VMEM((COLS * ROWS_PAD, 128), F32),
             pltpu.VMEM((64, 48, LANES), BF16),
@@ -344,7 +396,10 @@
             pltpu.VMEM((128, 128), F32),
             pltpu.VMEM((8, 256, 128), F32),
             pltpu.VMEM((8, 184, 128), F32),
+            pltpu.VMEM((ROWS, COLS, 128), BF16),
             pltpu.SemaphoreType.DMA,
+            pltpu.SemaphoreType.DMA((2,)),
+            pltpu.SemaphoreType.DMA((2,)),
             pltpu.SemaphoreType.DMA,
             pltpu.SemaphoreType.DMA((16,)),
             pltpu.SemaphoreType.DMA((8,)),
@@ -355,6 +410,7 @@
             pltpu.SemaphoreType.DMA((3,)),
             pltpu.SemaphoreType.DMA((3,)),
             pltpu.SemaphoreType.DMA((3,)),
+            pltpu.SemaphoreType.DMA((3,)),
         ],
         compiler_params=pltpu.CompilerParams(
             collective_id=0, has_side_effects=True, vmem_limit_bytes=VMEM_LIMIT
@@ -363,11 +419,30 @@
     )(*args)
 
 
+def copy_kernel(src_ref, dst_ref, sems):
+    copies = [pltpu.make_async_copy(src_ref.at[i], dst_ref.at[i], sems.at[i]) for i in range(ROWS)]
+    for copy in copies:
+        copy.start()
+    for copy in copies:
+        copy.wait()
+
+
+def copy_out(x):
+    return pl.pallas_call(
+        copy_kernel,
+        out_shape=jax.ShapeDtypeStruct(x.shape, x.dtype),
+        in_specs=[pl.BlockSpec(memory_space=pl.ANY)],
+        out_specs=pl.BlockSpec(memory_space=pl.ANY),
+        scratch_shapes=[pltpu.SemaphoreType.DMA((ROWS,))],
+        name="copy_out",
+    )(x)
+
+
 def body(pair_map, in_gain, project_weight, gate_weight, out_gain, out_weight):
-    sibling = lax.ppermute(pair_map, "col", [(0, 1), (1, 0), (2, 3), (3, 2)])
-    return fused(
-        pair_map, sibling, in_gain.reshape(1, 128), project_weight, gate_weight, out_gain.reshape(1, 128), out_weight
+    update = fused(
+        pair_map, in_gain.reshape(1, 128), project_weight, gate_weight, out_gain.reshape(1, 128), out_weight
     )
+    return copy_out(update)
 
 
 def solution(mesh):

time: 88 us -> 112 us (1.27)
  Pallas kernels: 80.8 us -> 112 us
  local copies, waits for them, and re-layouts: 3.16 us -> 0 us
  waiting for transfers between devices: 2.42 us -> 0 us
  starting transfers between devices: 1.42 us -> 0 us
    pallas_call x0 -> x1, Pallas kernels: none -> 31.3 us  [copy_out(): pl.pallas_call(copy_kernel, out_shape=jax.ShapeDtypeStruct(x.shape, x.dty...]
    unnamed x3 -> x0, local copies, waits for them, and re-layouts: 3.16 us -> none
    ppermute x1 -> x0, waiting for transfers between devices: 2.42 us -> none  [body(): sibling = lax.ppermute(pair_map, 'col', [(0, 1), (1, 0), (2, 3), (3, 2)])]
    ppermute x1 -> x0, starting transfers between devices: 1.42 us -> none  [body(): sibling = lax.ppermute(pair_map, 'col', [(0, 1), (1, 0), (2, 3), (3, 2)])]
  transfers between devices with their start and end apart: 1 -> 0, of which waited for: 1 -> 0; matrix products, arithmetic and copies ran while one was open for 0% -> 0% of each run, Pallas kernels for 0% -> 0%
where the time goes in v4:
time: 112 us
  Pallas kernels  112 us (100%)
    pallas_call x1, Pallas kernels, fused(): pl.pallas_call(kernel, out_shape=jax.ShapeDtypeStruct((ROWS, COLS, 128),...  80.9 us
    pallas_call x1, Pallas kernels, copy_out(): pl.pallas_call(copy_kernel, out_shape=jax.ShapeDtypeStruct(x.shape, x.dty...  31.3 us

profile of v4, /device:TPU:1, one launch (start us, length us, event | category | flops | bytes accessed | tf_op | source)
XLA Modules:
  0.0 112.3 jit_solution(16163800485618167744)
XLA Ops:
  0.0 80.9 %triangle_update.1.src_ref = bf16[22,176,128]{2,1,0:T(8,128)(2,1)} custom-call(bf16[22,176,128]{2,1,0:T(8,128)(2,1)} %own_ref.1, f32[1,128]{1,0:T(1,128)} %bitcast.2, bf16[128,512]{1,0:T(8,128)(2,1)} %weight_ref.1, bf16[128,128]{1,0:T(8,128)(2,1)} %gate_weight_ref.1, f32[1,128]{1,0:T(1,128)} %bitcast.3, bf16[128,128]{1,0:T(8,128)(2,1)} %out_weight_ref.1), custom_call_target="tpu_custom_call" | custom-call | tf_op jit(solution)/shard_map/triangle_update/pallas_call | solution.py:370
  81.0 31.3 %copy_out.1 = bf16[22,176,128]{2,1,0:T(8,128)(2,1)} custom-call(bf16[22,176,128]{2,1,0:T(8,128)(2,1)} %triangle_update.1.src_ref), custom_call_target="tpu_custom_call" | custom-call | tf_op jit(solution)/shard_map/copy_out/pallas_call | solution.py:431

commit v5 on v3

--- a/solution.py
+++ b/solution.py
@@ -74,9 +74,9 @@
 
 
 def kernel(
-    own_ref, sib_ref, gain_ref, weight_ref, gate_weight_ref, out_gain_ref, out_weight_ref, out_ref,
-    own, wt, normed, lr32, g32, lr, g, g_relay, lr_in, g_in, left, right, p, p_in, p_sib, p32, gates, gains, ws, mixed, packed,
-    own_sem, lr_send, lr_recv, g_send, g_recv, relay_send, relay_recv, p_send, p_recv, sib_send, sib_recv,
+    own_ref, gain_ref, weight_ref, gate_weight_ref, out_gain_ref, out_weight_ref, out_ref,
+    own, wt, main, rest, main32, rest32, g32, lr, g, g_relay, lr_in, g_in, left, right, p, p_in, p_sib, p32, gates, gains, ws, mixed, packed,
+    own_sem, map_send, map_recv, lr_send, lr_recv, g_send, g_recv, relay_send, relay_recv, p_send, p_recv, sib_send, sib_recv,
 ):
     row, col = place()
     half = col % 2
@@ -100,13 +100,9 @@
 
     signal(sibling)
     for hop in HOPS:
-        signal(chip_at(row, col, hop)[0])
-    for n in range(4):
-        signal({"row": 8 * ((col + 2) % 4) + 4 * y_hi + n, "col": z})
-
-        @pl.when(jnp.logical_or(jnp.logical_not(is_own), n != x))
-        def _():
-            signal({"row": base + n, "col": z})
+        device, _ = chip_at(row, col, hop)
+        signal(device)
+        signal({"row": device["row"], "col": device["col"] + 1 - 2 * half})
 
     own_copy = pltpu.make_async_copy(own_ref, own, own_sem)
     own_copy.start()
@@ -114,38 +110,100 @@
     wt[...] = weight_ref[...].astype(F32).T
     parts = [wt[pl.ds(pl.multiple_of(128 * n + HALF * half, HALF), HALF), :] for n in range(4)]
     weight = jnp.concatenate(parts, axis=0).astype(BF16)
+    weight_all = wt[...].astype(BF16)
     ones = jnp.full((128, 128), 1.0 / 128, BF16)
-    for i in range(ROWS):
-        normed[i, 2 * COLS :, :] = jnp.zeros((LANES - 2 * COLS, 128), BF16)
+    rest[:, 96:128, :] = jnp.zeros((ROWS, 32, 128), BF16)
     for pad in (22, 23, 46, 47):
-        for t in range(3):
-            lr32[t, pl.ds(pad, HALF, stride=48), :] = jnp.zeros((HALF, 128), F32)
+        main32[pl.ds(pad, CHANNELS, stride=48), :] = jnp.zeros((CHANNELS, 128), F32)
+        rest32[pl.ds(pad, HALF, stride=48), :] = jnp.zeros((HALF, 128), F32)
     for pad in (22, 23):
         g32[pl.ds(pad, COLS, stride=ROWS_PAD), :] = jnp.zeros((COLS, 128), F32)
+
     own_copy.wait()
 
     @pl.loop(0, 2)
     def _(n):
         for u in range(11):
             i = 11 * n + u
-            v = jnp.concatenate([own[i], sib_ref[i]], axis=0)
+            v = own[i]
             center = v.astype(F32) - jnp.dot(v, ones, preferred_element_type=F32)
             spread = jnp.dot((center * center).astype(BF16), ones, preferred_element_type=F32)
             y = center * lax.rsqrt(spread + 1e-05) * gain_ref[...]
-            normed[i, 0 : 2 * COLS, :] = y.astype(BF16)
-            g32[pl.ds(i, COLS, stride=ROWS_PAD), :] = y[0:COLS]
+            main[i] = y[0:128].astype(BF16)
+            rest[i, 0:48, :] = y[128:176].astype(BF16)
+            g32[pl.ds(i, COLS, stride=ROWS_PAD), :] = y
+
+    def factors(target, rows, n, weights, normed):
+        projected = lax.dot_general(weights, normed.reshape(256, 128), NT, preferred_element_type=F32)
+        one = sigmoid(projected[0:rows]) * projected[rows : 2 * rows]
+        two = sigmoid(projected[2 * rows : 3 * rows]) * projected[3 * rows :]
+        for u in range(2):
+            lanes = slice(128 * u, 128 * (u + 1))
+            target[pl.ds(2 * n + u, rows, stride=48), :] = one[:, lanes]
+            target[pl.ds(24 + 2 * n + u, rows, stride=48), :] = two[:, lanes]
+
+    for n in range(11):
+        factors(main32, CHANNELS, n, weight_all, main[2 * n : 2 * n + 2])
+
+    pl.semaphore_wait(barrier, 127)
+
+    swap_rest = pltpu.make_async_remote_copy(
+        src_ref=rest.at[:, pl.ds(0, 48), :],
+        dst_ref=rest.at[:, pl.ds(48, 48), :],
+        send_sem=map_send,
+        recv_sem=map_recv,
+        device_id=sibling,
+        device_id_type=MESH,
+    )
+    swap_rest.start()
+
+    def pack(source, channel):
+        return source[pl.ds(pl.multiple_of(channel * 48, 48), 48), :].astype(BF16)
+
+    def send_main(device, channel):
+        lr[channel] = pack(main32, channel)
+        pltpu.make_async_remote_copy(
+            src_ref=lr.at[channel],
+            dst_ref=lr_in.at[me, half],
+            send_sem=lr_send.at[0],
+            recv_sem=lr_recv.at[row // 2],
+            device_id=device,
+            device_id_type=MESH,
+        ).start()
+
+    for hop in HOPS:
+        device, chip = chip_at(row, col, hop)
+        send_main(device, HALF * half + chip)
+        send_main({"row": device["row"], "col": device["col"] + 1 - 2 * half}, HALF - HALF * half + chip)
+    send_main(sibling, HALF - HALF * half + me)
+    lr[HALF * half + me] = pack(main32, HALF * half + me)
+    pltpu.make_async_copy(lr.at[HALF * half + me], lr_in.at[me, half], lr_recv.at[row // 2]).start()
+
+    swap_rest.wait()
+    for n in range(11):
+        factors(rest32, HALF, n, weight, rest[2 * n : 2 * n + 2])
+    for hop in HOPS:
+        device, chip = chip_at(row, col, hop)
+        lr[CHANNELS + chip] = pack(rest32, chip)
+        pltpu.make_async_remote_copy(
+            src_ref=lr.at[CHANNELS + chip],
+            dst_ref=lr_in.at[me, 2],
+            send_sem=lr_send.at[1],
+            recv_sem=lr_recv.at[row // 2],
+            device_id=device,
+            device_id_type=MESH,
+        ).start()
+    lr[CHANNELS + me] = pack(rest32, me)
+    pltpu.make_async_copy(lr.at[CHANNELS + me], lr_in.at[me, 2], lr_recv.at[row // 2]).start()
 
     def pack_pairs(v):
         for n in range(2):
             rows = pl.ds(pl.multiple_of((22 * v + 11 * n) * ROWS_PAD, 8), 11 * ROWS_PAD)
             g[v, pl.ds(11 * n, 11)] = g32[rows, :].reshape(11, ROWS_PAD, 128).astype(BF16)
 
-    for v, _ in relays:
+    for n in range(4):
+        v, device = relays[n]
         pack_pairs(v)
-
-    pl.semaphore_wait(barrier, 72 - is_own.astype(jnp.int32))
-
-    for v, device in relays:
         pltpu.make_async_remote_copy(
             src_ref=g.at[v],
             dst_ref=g_relay.at[x],
@@ -155,38 +213,8 @@
             device_id_type=MESH,
         ).start()
 
-    @pl.loop(0, 2)
-    def _(n):
-        for u in range(11):
-            i = 11 * n + u
-            projected = lax.dot_general(weight, normed[i], NT, preferred_element_type=F32)
-            one = sigmoid(projected[0:64]) * projected[64:128]
-            two = sigmoid(projected[128:192]) * projected[192:256]
-            for t in range(3):
-                tile = slice(128 * t, 128 * (t + 1))
-                lr32[t, pl.ds(i, HALF, stride=48), :] = one[:, tile]
-                lr32[t, pl.ds(24 + i, HALF, stride=48), :] = two[:, tile]
-
-    def pack_factors(chip):
-        rows = pl.ds(pl.multiple_of(chip * 48, 48), 48)
-        for t in range(3):
-            lr[chip, :, 128 * t : 128 * (t + 1)] = lr32[t, rows, :].astype(BF16)
-
-    for hop in HOPS:
-        device, chip = chip_at(row, col, hop)
-        pack_factors(chip)
-        pltpu.make_async_remote_copy(
-            src_ref=lr.at[chip],
-            dst_ref=lr_in.at[me],
-            send_sem=lr_send,
-            recv_sem=lr_recv.at[row // 2],
-            device_id=device,
-            device_id_type=MESH,
-        ).start()
-    pack_factors(me)
-    pltpu.make_async_copy(lr.at[me], lr_in.at[me], lr_recv.at[row // 2]).start()
-
-    for n, (v, device) in enumerate(owners):
+        m = (n + 1) % 4
+        v, device = owners[m]
         pack_pairs(v)
 
         def send_pairs():
@@ -199,7 +227,7 @@
                 device_id_type=MESH,
             ).start()
 
-        if n == 0:
+        if m == 0:
 
             @pl.when(is_own)
             def _():
@@ -209,7 +237,7 @@
         else:
             send_pairs()
 
-    for n in range(4):
+    def send_on(n):
         s = (x + 4 - n) % 4
         wait_bytes(g_relay.at[s], relay_recv.at[s])
         pltpu.make_async_remote_copy(
@@ -226,12 +254,13 @@
         b = (row // 2 + n) % 16
         wait_bytes(lr_in.at[pl.ds(pl.multiple_of(4 * b, 4), 4)], lr_recv.at[b])
         for low in range(2):
-            one = lr_in[4 * b + low].astype(F32)
-            two = lr_in[4 * b + 2 + low].astype(F32)
-            rows = pl.ds(pl.multiple_of(48 * b, 48), 48)
-            lanes = slice(LANES * low, LANES * (low + 1))
-            left[rows, lanes] = jnp.concatenate([one[:24], two[:24]], axis=0).astype(BF16)
-            right[rows, lanes] = jnp.concatenate([one[24:], two[24:]], axis=0).astype(BF16)
+            for t in range(3):
+                one = lr_in[4 * b + low, t].astype(F32)
+                two = lr_in[4 * b + 2 + low, t].astype(F32)
+                rows = pl.ds(pl.multiple_of(48 * b, 48), 48)
+                lanes = slice(LANES * low + 128 * t, LANES * low + 128 * (t + 1))
+                left[rows, lanes] = jnp.concatenate([one[:24], two[:24]], axis=0).astype(BF16)
+                right[rows, lanes] = jnp.concatenate([one[24:], two[24:]], axis=0).astype(BF16)
 
     for n in range(2):
         acc = lax.dot_general(right[384 * n : 384 * (n + 1), :], left[...], NT, preferred_element_type=F32)
@@ -254,6 +283,9 @@
                 device_id=device,
                 device_id_type=MESH,
             ).start()
+        if k == 0:
+            for n in range(4):
+                send_on(n)
 
     for s in range(8):
         wait_bytes(g_in.at[s], g_recv.at[s])
@@ -267,11 +299,11 @@
 
     gains[...] = jnp.broadcast_to(out_gain_ref[...], (128, 128)).T
     ws[...] = out_weight_ref[...].astype(F32)
-    first = pl.ds(pl.multiple_of(HALF * half, HALF), HALF)
-    second = pl.ds(pl.multiple_of(HALF - HALF * half, HALF), HALF)
-    gain = jnp.concatenate([gains[first, :], gains[second, :]], axis=0)
+    ours = pl.ds(pl.multiple_of(HALF * half, HALF), HALF)
+    theirs = pl.ds(pl.multiple_of(HALF - HALF * half, HALF), HALF)
+    gain = jnp.concatenate([gains[ours, :], gains[theirs, :]], axis=0)
     gain = jnp.concatenate([gain, gain], axis=1)
-    out_weight = jnp.concatenate([ws[first, :], ws[second, :]], axis=0).astype(BF16)
+    out_weight = jnp.concatenate([ws[ours, :], ws[theirs, :]], axis=0).astype(BF16)
 
     for k, (start, stop) in enumerate(GROUPS):
         wait_bytes(p_in.at[k], p_recv.at[k])
@@ -302,7 +334,8 @@
                 packed[u, 22 * s : 22 * s + 24, :] = update[24 * s : 24 * s + 24]
             out_ref[j] = packed[u, 0:COLS, :].astype(BF16)
 
-    wait_bytes(lr.at[pl.ds(0, 63)], lr_send)
+    wait_bytes(lr.at[pl.ds(0, 127)], lr_send.at[0])
+    wait_bytes(lr.at[pl.ds(0, 63)], lr_send.at[1])
     for k in range(3):
         wait_bytes(p.at[k, pl.ds(0, 63)], p_send.at[k])
     for v, _ in relays + owners[1:]:
@@ -320,18 +353,20 @@
     return pl.pallas_call(
         kernel,
         out_shape=jax.ShapeDtypeStruct((ROWS, COLS, 128), BF16),
-        in_specs=[pl.BlockSpec(memory_space=pl.ANY)] + [vmem] * 6,
+        in_specs=[pl.BlockSpec(memory_space=pl.ANY)] + [vmem] * 5,
         out_specs=vmem,
         scratch_shapes=[
             pltpu.VMEM((ROWS, COLS, 128), BF16),
             pltpu.VMEM((512, 128), F32),
-            pltpu.VMEM((ROWS, LANES, 128), BF16),
-            pltpu.VMEM((3, HALF * 48, 128), F32),
+            pltpu.VMEM((ROWS, 128, 128), BF16),
+            pltpu.VMEM((ROWS, 128, 128), BF16),
+            pltpu.VMEM((CHANNELS * 48, 128), F32),
+            pltpu.VMEM((HALF * 48, 128), F32),
             pltpu.VMEM((COLS * ROWS_PAD, 128), F32),
-            pltpu.VMEM((64, 48, LANES), BF16),
+            pltpu.VMEM((CHANNELS + HALF, 48, 128), BF16),
             pltpu.VMEM((8, ROWS, ROWS_PAD, 128), BF16),
             pltpu.VMEM((4, ROWS, ROWS_PAD, 128), BF16),
-            pltpu.VMEM((64, 48, LANES), BF16),
+            pltpu.VMEM((64, 3, 48, 128), BF16),
             pltpu.VMEM((8, ROWS, ROWS_PAD, 128), BF16),
             pltpu.VMEM((768, 768), BF16),
             pltpu.VMEM((768, 768), BF16),
@@ -346,6 +381,8 @@
             pltpu.VMEM((8, 184, 128), F32),
             pltpu.SemaphoreType.DMA,
             pltpu.SemaphoreType.DMA,
+            pltpu.SemaphoreType.DMA,
+            pltpu.SemaphoreType.DMA((2,)),
             pltpu.SemaphoreType.DMA((16,)),
             pltpu.SemaphoreType.DMA((8,)),
             pltpu.SemaphoreType.DMA((8,)),
@@ -363,11 +400,30 @@
     )(*args)
 
 
+def copy_kernel(src_ref, dst_ref, sems):
+    copies = [pltpu.make_async_copy(src_ref.at[i], dst_ref.at[i], sems.at[i]) for i in range(ROWS)]
+    for copy in copies:
+        copy.start()
+    for copy in copies:
+        copy.wait()
+
+
+def copy_out(x):
+    return pl.pallas_call(
+        copy_kernel,
+        out_shape=jax.ShapeDtypeStruct(x.shape, x.dtype),
+        in_specs=[pl.BlockSpec(memory_space=pltpu.VMEM)],
+        out_specs=pl.BlockSpec(memory_space=pl.ANY),
+        scratch_shapes=[pltpu.SemaphoreType.DMA((ROWS,))],
+        name="copy_out",
+    )(x)
+
+
 def body(pair_map, in_gain, project_weight, gate_weight, out_gain, out_weight):
-    sibling = lax.ppermute(pair_map, "col", [(0, 1), (1, 0), (2, 3), (3, 2)])
-    return fused(
-        pair_map, sibling, in_gain.reshape(1, 128), project_weight, gate_weight, out_gain.reshape(1, 128), out_weight
+    update = fused(
+        pair_map, in_gain.reshape(1, 128), project_weight, gate_weight, out_gain.reshape(1, 128), out_weight
     )
+    return copy_out(update)
 
 
 def solution(mesh):

time: 88 us -> 83.7 us (0.951)
  the two profiles are of different devices: /device:TPU:1 before, /device:TPU:35 now
where the time goes in v5:
time: 83.7 us; the launch traced here: 83.5 us
  Pallas kernels  83.5 us (100%)
    pallas_call x1, Pallas kernels, fused(): pl.pallas_call(kernel, out_shape=jax.ShapeDtypeStruct((ROWS, COLS, 128),...  81.2 us
    pallas_call x1, Pallas kernels, copy_out(): pl.pallas_call(copy_kernel, out_shape=jax.ShapeDtypeStruct(x.shape, x.dty...  2.33 us

profile of v5, /device:TPU:35, one launch (start us, length us, event | category | flops | bytes accessed | tf_op | source)
XLA Modules:
  0.0 83.5 jit_solution(11282846160285983806)
XLA Ops:
  0.0 81.2 %triangle_update.1.src_ref = bf16[22,176,128]{2,1,0:T(8,128)(2,1)} custom-call(bf16[22,176,128]{2,1,0:T(8,128)(2,1)} %own_ref.1, f32[1,128]{1,0:T(1,128)} %bitcast.2, bf16[128,512]{1,0:T(8,128)(2,1)} %weight_ref.1, bf16[128,128]{1,0:T(8,128)(2,1)} %gate_weight_ref.1, f32[1,128]{1,0:T(1,128)} %bitcast.3, bf16[128,128]{1,0:T(8,128)(2,1)} %out_weight_ref.1), custom_call_target="tpu_custom_call" | custom-call | tf_op jit(solution)/shard_map/triangle_update/pallas_call | solution.py:353
  81.2 2.3 %copy_out.1 = bf16[22,176,128]{2,1,0:T(8,128)(2,1)} custom-call(bf16[22,176,128]{2,1,0:T(8,128)(2,1)} %triangle_update.1.src_ref), custom_call_target="tpu_custom_call" | custom-call | tf_op jit(solution)/shard_map/copy_out/pallas_call | solution.py:412

commit v6 on v5

--- a/solution.py
+++ b/solution.py
@@ -142,6 +142,61 @@
             target[pl.ds(2 * n + u, rows, stride=48), :] = one[:, lanes]
             target[pl.ds(24 + 2 * n + u, rows, stride=48), :] = two[:, lanes]
 
+    def pack_pairs(v):
+        for n in range(2):
+            rows = pl.ds(pl.multiple_of((22 * v + 11 * n) * ROWS_PAD, 8), 11 * ROWS_PAD)
+            g[v, pl.ds(11 * n, 11)] = g32[rows, :].reshape(11, ROWS_PAD, 128).astype(BF16)
+
+    def send_pairs(n):
+        v, device = relays[n]
+        pltpu.make_async_remote_copy(
+            src_ref=g.at[v],
+            dst_ref=g_relay.at[x],
+            send_sem=g_send.at[v],
+            recv_sem=relay_recv.at[x],
+            device_id=device,
+            device_id_type=MESH,
+        ).start()
+
+        m = (n + 2) % 4
+        v2, device2 = owners[m]
+
+        def send_direct():
+            pltpu.make_async_remote_copy(
+                src_ref=g.at[v2],
+                dst_ref=g_in.at[row % 8],
+                send_sem=g_send.at[v2],
+                recv_sem=g_recv.at[row % 8],
+                device_id=device2,
+                device_id_type=MESH,
+            ).start()
+
+        if m == 0:
+
+            @pl.when(is_own)
+            def _():
+                pltpu.make_async_copy(g.at[v2], g_in.at[v2], g_recv.at[v2]).start()
+
+            pl.when(jnp.logical_not(is_own))(send_direct)
+        else:
+            send_direct()
+
+    def send_on(n):
+        s = (x + 4 - n) % 4
+        wait_bytes(g_relay.at[s], relay_recv.at[s])
+        pltpu.make_async_remote_copy(
+            src_ref=g_relay.at[s],
+            dst_ref=g_in.at[4 * y_hi + s],
+            send_sem=relay_send.at[s],
+            recv_sem=g_recv.at[4 * y_hi + s],
+            device_id=forward,
+            device_id_type=MESH,
+        ).start()
+
+    for n in (0, 1):
+        pack_pairs(relays[n][0])
+        pack_pairs(owners[(n + 2) % 4][0])
+
     for n in range(11):
         factors(main32, CHANNELS, n, weight_all, main[2 * n : 2 * n + 2])
 
@@ -156,6 +211,7 @@
         device_id_type=MESH,
     )
     swap_rest.start()
+    send_pairs(0)
 
     def pack(source, channel):
         return source[pl.ds(pl.multiple_of(channel * 48, 48), 48), :].astype(BF16)
@@ -179,6 +235,7 @@
     lr[HALF * half + me] = pack(main32, HALF * half + me)
     pltpu.make_async_copy(lr.at[HALF * half + me], lr_in.at[me, half], lr_recv.at[row // 2]).start()
 
+    send_pairs(1)
     swap_rest.wait()
     for n in range(11):
         factors(rest32, HALF, n, weight, rest[2 * n : 2 * n + 2])
@@ -196,82 +253,37 @@
     lr[CHANNELS + me] = pack(rest32, me)
     pltpu.make_async_copy(lr.at[CHANNELS + me], lr_in.at[me, 2], lr_recv.at[row // 2]).start()
 
-    def pack_pairs(v):
-        for n in range(2):
-            rows = pl.ds(pl.multiple_of((22 * v + 11 * n) * ROWS_PAD, 8), 11 * ROWS_PAD)
-            g[v, pl.ds(11 * n, 11)] = g32[rows, :].reshape(11, ROWS_PAD, 128).astype(BF16)
-
-    for n in range(4):
-        v, device = relays[n]
-        pack_pairs(v)
-        pltpu.make_async_remote_copy(
-            src_ref=g.at[v],
-            dst_ref=g_relay.at[x],
-            send_sem=g_send.at[v],
-            recv_sem=relay_recv.at[x],
-            device_id=device,
-            device_id_type=MESH,
-        ).start()
-
-        m = (n + 1) % 4
-        v, device = owners[m]
-        pack_pairs(v)
-
-        def send_pairs():
-            pltpu.make_async_remote_copy(
-                src_ref=g.at[v],
-                dst_ref=g_in.at[row % 8],
-                send_sem=g_send.at[v],
-                recv_sem=g_recv.at[row % 8],
-                device_id=device,
-                device_id_type=MESH,
-            ).start()
-
-        if m == 0:
-
-            @pl.when(is_own)
-            def _():
-                pltpu.make_async_copy(g.at[v], g_in.at[v], g_recv.at[v]).start()
-
-            pl.when(jnp.logical_not(is_own))(send_pairs)
-        else:
-            send_pairs()
-
-    def send_on(n):
-        s = (x + 4 - n) % 4
-        wait_bytes(g_relay.at[s], relay_recv.at[s])
-        pltpu.make_async_remote_copy(
-            src_ref=g_relay.at[s],
-            dst_ref=g_in.at[4 * y_hi + s],
-            send_sem=relay_send.at[s],
-            recv_sem=g_recv.at[4 * y_hi + s],
-            device_id=forward,
-            device_id_type=MESH,
-        ).start()
-
-    @pl.loop(0, BLOCKS // 2)
-    def _(n):
+    send_on(0)
+    for n in (2, 3):
+        pack_pairs(relays[n][0])
+        pack_pairs(owners[(n + 2) % 4][0])
+        send_pairs(n)
+
+    def take(n):
         b = (row // 2 + n) % 16
         wait_bytes(lr_in.at[pl.ds(pl.multiple_of(4 * b, 4), 4)], lr_recv.at[b])
+        rows = pl.ds(pl.multiple_of(48 * b, 48), 48)
         for low in range(2):
             for t in range(3):
                 one = lr_in[4 * b + low, t].astype(F32)
                 two = lr_in[4 * b + 2 + low, t].astype(F32)
-                rows = pl.ds(pl.multiple_of(48 * b, 48), 48)
                 lanes = slice(LANES * low + 128 * t, LANES * low + 128 * (t + 1))
                 left[rows, lanes] = jnp.concatenate([one[:24], two[:24]], axis=0).astype(BF16)
-                right[rows, lanes] = jnp.concatenate([one[24:], two[24:]], axis=0).astype(BF16)
-
-    for n in range(2):
-        acc = lax.dot_general(right[384 * n : 384 * (n + 1), :], left[...], NT, preferred_element_type=F32)
-        for b in range(16):
+                for k in range(3):
+                    part = slice(24 + 8 * k, 32 + 8 * k)
+                    right[pl.ds(pl.multiple_of(256 * k + 16 * b, 16), 16), lanes] = jnp.concatenate(
+                        [one[part], two[part]], axis=0
+                    ).astype(BF16)
+
+    pl.loop(0, 8)(take)
+    send_on(1)
+    pl.loop(8, 16)(take)
+
+    for k in range(3):
+        acc = lax.dot_general(right[256 * k : 256 * (k + 1), :], left[...], NT, preferred_element_type=F32)
+        for r in range(BLOCKS):
             for low in range(2):
-                for k in range(3):
-                    p[k, 32 * n + 2 * b + low] = acc[
-                        24 * b + 8 * k : 24 * b + 8 * k + 8, LANES * low : LANES * (low + 1)
-                    ].astype(BF16)
-
-    for k in range(3):
+                p[k, 2 * r + low] = acc[8 * r : 8 * r + 8, LANES * low : LANES * (low + 1)].astype(BF16)
         pltpu.make_async_copy(p.at[k, me], p_in.at[k, me], p_recv.at[k]).start()
         for hop in HOPS:
             device, chip = chip_at(row, col, hop)
@@ -283,9 +295,8 @@
                 device_id=device,
                 device_id_type=MESH,
             ).start()
-        if k == 0:
-            for n in range(4):
-                send_on(n)
+        if k < 2:
+            send_on(k + 2)
 
     for s in range(8):
         wait_bytes(g_in.at[s], g_recv.at[s])
@@ -400,11 +411,15 @@
     )(*args)
 
 
-def copy_kernel(src_ref, dst_ref, sems):
-    copies = [pltpu.make_async_copy(src_ref.at[i], dst_ref.at[i], sems.at[i]) for i in range(ROWS)]
-    for copy in copies:
+def copy_kernel(src_ref, dst_ref, held, in_sems, out_sems):
+    ins = [pltpu.make_async_copy(src_ref.at[i], held.at[i], in_sems.at[i]) for i in range(ROWS)]
+    outs = [pltpu.make_async_copy(held.at[i], dst_ref.at[i], out_sems.at[i]) for i in range(ROWS)]
+    for copy in ins:
         copy.start()
-    for copy in copies:
+    for i in range(ROWS):
+        ins[i].wait()
+        outs[i].start()
+    for copy in outs:
         copy.wait()
 
 
@@ -412,9 +427,13 @@
     return pl.pallas_call(
         copy_kernel,
         out_shape=jax.ShapeDtypeStruct(x.shape, x.dtype),
-        in_specs=[pl.BlockSpec(memory_space=pltpu.VMEM)],
+        in_specs=[pl.BlockSpec(memory_space=pl.ANY)],
         out_specs=pl.BlockSpec(memory_space=pl.ANY),
-        scratch_shapes=[pltpu.SemaphoreType.DMA((ROWS,))],
+        scratch_shapes=[
+            pltpu.VMEM(x.shape, x.dtype),
+            pltpu.SemaphoreType.DMA((ROWS,)),
+            pltpu.SemaphoreType.DMA((ROWS,)),
+        ],
         name="copy_out",
     )(x)
 

time: 83.7 us -> 80.2 us (0.958)
  the two profiles are of different devices: /device:TPU:35 before, /device:TPU:1 now
where the time goes in v6:
time: 80.2 us; the launch traced here: 80 us
  Pallas kernels  80 us (100%)
    pallas_call x1, Pallas kernels, fused(): pl.pallas_call(kernel, out_shape=jax.ShapeDtypeStruct((ROWS, COLS, 128),...  77.8 us
    pallas_call x1, Pallas kernels, copy_out(): pl.pallas_call(copy_kernel, out_shape=jax.ShapeDtypeStruct(x.shape, x.dty...  2.19 us

profile of v6, /device:TPU:1, one launch (start us, length us, event | category | flops | bytes accessed | tf_op | source)
XLA Modules:
  0.0 80.0 jit_solution(571836478516588787)
XLA Ops:
  0.0 77.8 %triangle_update.1.src_ref = bf16[22,176,128]{2,1,0:T(8,128)(2,1)} custom-call(bf16[22,176,128]{2,1,0:T(8,128)(2,1)} %own_ref.1, f32[1,128]{1,0:T(1,128)} %bitcast.2, bf16[128,512]{1,0:T(8,128)(2,1)} %weight_ref.1, bf16[128,128]{1,0:T(8,128)(2,1)} %gate_weight_ref.1, f32[1,128]{1,0:T(1,128)} %bitcast.3, bf16[128,128]{1,0:T(8,128)(2,1)} %out_weight_ref.1), custom_call_target="tpu_custom_call" | custom-call | tf_op jit(solution)/shard_map/triangle_update/pallas_call | solution.py:364
  77.8 2.2 %copy_out.1 = bf16[22,176,128]{2,1,0:T(8,128)(2,1)} custom-call(bf16[22,176,128]{2,1,0:T(8,128)(2,1)} %triangle_update.1.src_ref), custom_call_target="tpu_custom_call" | custom-call | tf_op jit(solution)/shard_map/copy_out/pallas_call | solution.py:427

commit v7 on v6

--- a/solution.py
+++ b/solution.py
@@ -75,8 +75,8 @@
 
 def kernel(
     own_ref, gain_ref, weight_ref, gate_weight_ref, out_gain_ref, out_weight_ref, out_ref,
-    own, wt, main, rest, main32, rest32, g32, lr, g, g_relay, lr_in, g_in, left, right, p, p_in, p_sib, p32, gates, gains, ws, mixed, packed,
-    own_sem, map_send, map_recv, lr_send, lr_recv, g_send, g_recv, relay_send, relay_recv, p_send, p_recv, sib_send, sib_recv,
+    own, wt, main, rest, main32, rest32, g32, lr_a, lr_b, g, g_relay, lr_a_in, lr_b_in, g_in, left, right, p, p_in, p_sib, p32, gates, gains, ws, mixed, packed,
+    own_sem, map_send, map_recv, lr_send, lr_a_recv, lr_b_recv, g_send, g_recv, relay_send, relay_recv, p_send, p_recv, sib_send, sib_recv,
 ):
     row, col = place()
     half = col % 2
@@ -211,75 +211,80 @@
         device_id_type=MESH,
     )
     swap_rest.start()
+
+    parts = ((lr_a, lr_a_in, 0, 32, lr_a_recv), (lr_b, lr_b_in, 32, 16, lr_b_recv))
+
+    def send_factors(part, source, channel, slot, device, kind):
+        buffer, landing, start, rows, recv = parts[part]
+        index = channel if kind < 2 else CHANNELS + channel
+        buffer[index] = source[pl.ds(pl.multiple_of(channel * 48 + start, 16), rows), :].astype(BF16)
+        if device is None:
+            pltpu.make_async_copy(buffer.at[index], landing.at[me, slot], recv.at[row // 2]).start()
+        else:
+            pltpu.make_async_remote_copy(
+                src_ref=buffer.at[index],
+                dst_ref=landing.at[me, slot],
+                send_sem=lr_send.at[part],
+                recv_sem=recv.at[row // 2],
+                device_id=device,
+                device_id_type=MESH,
+            ).start()
+
+    def send_main(part):
+        for hop in HOPS:
+            device, chip = chip_at(row, col, hop)
+            send_factors(part, main32, HALF * half + chip, half, device, 0)
+            across = {"row": device["row"], "col": device["col"] + 1 - 2 * half}
+            send_factors(part, main32, HALF - HALF * half + chip, half, across, 1)
+        send_factors(part, main32, HALF - HALF * half + me, half, sibling, 1)
+        send_factors(part, main32, HALF * half + me, half, None, 0)
+
+    def send_rest(part):
+        for hop in HOPS:
+            device, chip = chip_at(row, col, hop)
+            send_factors(part, rest32, chip, 2, device, 2)
+        send_factors(part, rest32, me, 2, None, 2)
+
+    send_main(0)
     send_pairs(0)
-
-    def pack(source, channel):
-        return source[pl.ds(pl.multiple_of(channel * 48, 48), 48), :].astype(BF16)
-
-    def send_main(device, channel):
-        lr[channel] = pack(main32, channel)
-        pltpu.make_async_remote_copy(
-            src_ref=lr.at[channel],
-            dst_ref=lr_in.at[me, half],
-            send_sem=lr_send.at[0],
-            recv_sem=lr_recv.at[row // 2],
-            device_id=device,
-            device_id_type=MESH,
-        ).start()
-
-    for hop in HOPS:
-        device, chip = chip_at(row, col, hop)
-        send_main(device, HALF * half + chip)
-        send_main({"row": device["row"], "col": device["col"] + 1 - 2 * half}, HALF - HALF * half + chip)
-    send_main(sibling, HALF - HALF * half + me)
-    lr[HALF * half + me] = pack(main32, HALF * half + me)
-    pltpu.make_async_copy(lr.at[HALF * half + me], lr_in.at[me, half], lr_recv.at[row // 2]).start()
-
     send_pairs(1)
     swap_rest.wait()
     for n in range(11):
         factors(rest32, HALF, n, weight, rest[2 * n : 2 * n + 2])
-    for hop in HOPS:
-        device, chip = chip_at(row, col, hop)
-        lr[CHANNELS + chip] = pack(rest32, chip)
-        pltpu.make_async_remote_copy(
-            src_ref=lr.at[CHANNELS + chip],
-            dst_ref=lr_in.at[me, 2],
-            send_sem=lr_send.at[1],
-            recv_sem=lr_recv.at[row // 2],
-            device_id=device,
-            device_id_type=MESH,
-        ).start()
-    lr[CHANNELS + me] = pack(rest32, me)
-    pltpu.make_async_copy(lr.at[CHANNELS + me], lr_in.at[me, 2], lr_recv.at[row // 2]).start()
-
-    send_on(0)
+    send_rest(0)
     for n in (2, 3):
         pack_pairs(relays[n][0])
         pack_pairs(owners[(n + 2) % 4][0])
         send_pairs(n)
-
-    def take(n):
+    send_main(1)
+    send_rest(1)
+
+    def landed(part, n):
         b = (row // 2 + n) % 16
-        wait_bytes(lr_in.at[pl.ds(pl.multiple_of(4 * b, 4), 4)], lr_recv.at[b])
-        rows = pl.ds(pl.multiple_of(48 * b, 48), 48)
+        landing, recv = parts[part][1], parts[part][4]
+        wait_bytes(landing.at[pl.ds(pl.multiple_of(4 * b, 4), 4)], recv.at[b])
         for low in range(2):
             for t in range(3):
-                one = lr_in[4 * b + low, t].astype(F32)
-                two = lr_in[4 * b + 2 + low, t].astype(F32)
-                lanes = slice(LANES * low + 128 * t, LANES * low + 128 * (t + 1))
-                left[rows, lanes] = jnp.concatenate([one[:24], two[:24]], axis=0).astype(BF16)
-                for k in range(3):
-                    part = slice(24 + 8 * k, 32 + 8 * k)
-                    right[pl.ds(pl.multiple_of(256 * k + 16 * b, 16), 16), lanes] = jnp.concatenate(
-                        [one[part], two[part]], axis=0
-                    ).astype(BF16)
-
-    pl.loop(0, 8)(take)
-    send_on(1)
-    pl.loop(8, 16)(take)
-
-    for k in range(3):
+                one = landing[4 * b + low, t].astype(F32)
+                two = landing[4 * b + 2 + low, t].astype(F32)
+                yield b, slice(LANES * low + 128 * t, LANES * low + 128 * (t + 1)), one, two
+
+    def take_right(b, k, lanes, one, two):
+        rows = pl.ds(pl.multiple_of(256 * k + 16 * b, 16), 16)
+        right[rows, lanes] = jnp.concatenate([one, two], axis=0).astype(BF16)
+
+    def take_first(n):
+        for b, lanes, one, two in landed(0, n):
+            rows = pl.ds(pl.multiple_of(48 * b, 48), 48)
+            left[rows, lanes] = jnp.concatenate([one[:24], two[:24]], axis=0).astype(BF16)
+            take_right(b, 0, lanes, one[24:], two[24:])
+
+    def take_second(n):
+        for b, lanes, one, two in landed(1, n):
+            take_right(b, 1, lanes, one[:8], two[:8])
+            take_right(b, 2, lanes, one[8:], two[8:])
+
+    def send_products(k):
         acc = lax.dot_general(right[256 * k : 256 * (k + 1), :], left[...], NT, preferred_element_type=F32)
         for r in range(BLOCKS):
             for low in range(2):
@@ -295,8 +300,17 @@
                 device_id=device,
                 device_id_type=MESH,
             ).start()
-        if k < 2:
-            send_on(k + 2)
+
+    pl.loop(0, 8)(take_first)
+    send_on(0)
+    send_on(1)
+    pl.loop(8, 16)(take_first)
+    send_products(0)
+    send_on(2)
+    send_on(3)
+    pl.loop(0, 16)(take_second)
+    send_products(1)
+    send_products(2)
 
     for s in range(8):
         wait_bytes(g_in.at[s], g_recv.at[s])
@@ -345,8 +359,8 @@
                 packed[u, 22 * s : 22 * s + 24, :] = update[24 * s : 24 * s + 24]
             out_ref[j] = packed[u, 0:COLS, :].astype(BF16)
 
-    wait_bytes(lr.at[pl.ds(0, 127)], lr_send.at[0])
-    wait_bytes(lr.at[pl.ds(0, 63)], lr_send.at[1])
+    wait_bytes(lr_a.at[pl.ds(0, 190)], lr_send.at[0])
+    wait_bytes(lr_b.at[pl.ds(0, 190)], lr_send.at[1])
     for k in range(3):
         wait_bytes(p.at[k, pl.ds(0, 63)], p_send.at[k])
     for v, _ in relays + owners[1:]:
@@ -374,10 +388,12 @@
             pltpu.VMEM((CHANNELS * 48, 128), F32),
             pltpu.VMEM((HALF * 48, 128), F32),
             pltpu.VMEM((COLS * ROWS_PAD, 128), F32),
-            pltpu.VMEM((CHANNELS + HALF, 48, 128), BF16),
+            pltpu.VMEM((CHANNELS + HALF, 32, 128), BF16),
+            pltpu.VMEM((CHANNELS + HALF, 16, 128), BF16),
             pltpu.VMEM((8, ROWS, ROWS_PAD, 128), BF16),
             pltpu.VMEM((4, ROWS, ROWS_PAD, 128), BF16),
-            pltpu.VMEM((64, 3, 48, 128), BF16),
+            pltpu.VMEM((64, 3, 32, 128), BF16),
+            pltpu.VMEM((64, 3, 16, 128), BF16),
             pltpu.VMEM((8, ROWS, ROWS_PAD, 128), BF16),
             pltpu.VMEM((768, 768), BF16),
             pltpu.VMEM((768, 768), BF16),
@@ -395,6 +411,7 @@
             pltpu.SemaphoreType.DMA,
             pltpu.SemaphoreType.DMA((2,)),
             pltpu.SemaphoreType.DMA((16,)),
+            pltpu.SemaphoreType.DMA((16,)),
             pltpu.SemaphoreType.DMA((8,)),
             pltpu.SemaphoreType.DMA((8,)),
             pltpu.SemaphoreType.DMA((4,)),

time: 80.2 us -> 83.9 us (1.046)
  Pallas kernels: 80 us -> 83.7 us
    pallas_call x1, Pallas kernels: 77.8 us -> 81.5 us  [fused(): pl.pallas_call(kernel, out_shape=jax.ShapeDtypeStruct((ROWS, COLS, 128),...]
where the time goes in v7:
time: 83.9 us; the launch traced here: 83.7 us
  Pallas kernels  83.7 us (100%)
    pallas_call x1, Pallas kernels, fused(): pl.pallas_call(kernel, out_shape=jax.ShapeDtypeStruct((ROWS, COLS, 128),...  81.5 us
    pallas_call x1, Pallas kernels, copy_out(): pl.pallas_call(copy_kernel, out_shape=jax.ShapeDtypeStruct(x.shape, x.dty...  2.19 us

profile of v7, /device:TPU:1, one launch (start us, length us, event | category | flops | bytes accessed | tf_op | source)
XLA Modules:
  0.0 83.7 jit_solution(16002727287104501613)
XLA Ops:
  0.0 81.5 %triangle_update.1.src_ref = bf16[22,176,128]{2,1,0:T(8,128)(2,1)} custom-call(bf16[22,176,128]{2,1,0:T(8,128)(2,1)} %own_ref.1, f32[1,128]{1,0:T(1,128)} %bitcast.2, bf16[128,512]{1,0:T(8,128)(2,1)} %weight_ref.1, bf16[128,128]{1,0:T(8,128)(2,1)} %gate_weight_ref.1, f32[1,128]{1,0:T(1,128)} %bitcast.3, bf16[128,128]{1,0:T(8,128)(2,1)} %out_weight_ref.1), custom_call_target="tpu_custom_call" | custom-call | tf_op jit(solution)/shard_map/triangle_update/pallas_call | solution.py:378
  81.5 2.2 %copy_out.1 = bf16[22,176,128]{2,1,0:T(8,128)(2,1)} custom-call(bf16[22,176,128]{2,1,0:T(8,128)(2,1)} %triangle_update.1.src_ref), custom_call_target="tpu_custom_call" | custom-call | tf_op jit(solution)/shard_map/copy_out/pallas_call | solution.py:444

commit v8 on v7

--- a/solution.py
+++ b/solution.py
@@ -147,13 +147,14 @@
             rows = pl.ds(pl.multiple_of((22 * v + 11 * n) * ROWS_PAD, 8), 11 * ROWS_PAD)
             g[v, pl.ds(11 * n, 11)] = g32[rows, :].reshape(11, ROWS_PAD, 128).astype(BF16)
 
-    def send_pairs(n):
+    def send_pairs(step):
+        n, rows = step // 2, pl.ds(11 * (step % 2), 11)
         v, device = relays[n]
         pltpu.make_async_remote_copy(
-            src_ref=g.at[v],
-            dst_ref=g_relay.at[x],
+            src_ref=g.at[v, rows],
+            dst_ref=g_relay.at[x, rows],
             send_sem=g_send.at[v],
-            recv_sem=relay_recv.at[x],
+            recv_sem=relay_recv.at[x, step % 2],
             device_id=device,
             device_id_type=MESH,
         ).start()
@@ -163,8 +164,8 @@
 
         def send_direct():
             pltpu.make_async_remote_copy(
-                src_ref=g.at[v2],
-                dst_ref=g_in.at[row % 8],
+                src_ref=g.at[v2, rows],
+                dst_ref=g_in.at[row % 8, rows],
                 send_sem=g_send.at[v2],
                 recv_sem=g_recv.at[row % 8],
                 device_id=device2,
@@ -175,18 +176,18 @@
 
             @pl.when(is_own)
             def _():
-                pltpu.make_async_copy(g.at[v2], g_in.at[v2], g_recv.at[v2]).start()
+                pltpu.make_async_copy(g.at[v2, rows], g_in.at[v2, rows], g_recv.at[v2]).start()
 
             pl.when(jnp.logical_not(is_own))(send_direct)
         else:
             send_direct()
 
-    def send_on(n):
-        s = (x + 4 - n) % 4
-        wait_bytes(g_relay.at[s], relay_recv.at[s])
+    def send_on(step):
+        s, rows = (x + 4 - step // 2) % 4, pl.ds(11 * (step % 2), 11)
+        wait_bytes(g_relay.at[s, rows], relay_recv.at[s, step % 2])
         pltpu.make_async_remote_copy(
-            src_ref=g_relay.at[s],
-            dst_ref=g_in.at[4 * y_hi + s],
+            src_ref=g_relay.at[s, rows],
+            dst_ref=g_in.at[4 * y_hi + s, rows],
             send_sem=relay_send.at[s],
             recv_sem=g_recv.at[4 * y_hi + s],
             device_id=forward,
@@ -230,34 +231,43 @@
                 device_id_type=MESH,
             ).start()
 
-    def send_main(part):
-        for hop in HOPS:
+    def send_main(part, start, stop):
+        for hop in HOPS[start:stop]:
             device, chip = chip_at(row, col, hop)
             send_factors(part, main32, HALF * half + chip, half, device, 0)
             across = {"row": device["row"], "col": device["col"] + 1 - 2 * half}
             send_factors(part, main32, HALF - HALF * half + chip, half, across, 1)
-        send_factors(part, main32, HALF - HALF * half + me, half, sibling, 1)
-        send_factors(part, main32, HALF * half + me, half, None, 0)
-
-    def send_rest(part):
-        for hop in HOPS:
+        if start == 0:
+            send_factors(part, main32, HALF - HALF * half + me, half, sibling, 1)
+            send_factors(part, main32, HALF * half + me, half, None, 0)
+
+    def send_rest(part, start, stop):
+        for hop in HOPS[start:stop]:
             device, chip = chip_at(row, col, hop)
             send_factors(part, rest32, chip, 2, device, 2)
-        send_factors(part, rest32, me, 2, None, 2)
-
-    send_main(0)
-    send_pairs(0)
-    send_pairs(1)
-    swap_rest.wait()
-    for n in range(11):
-        factors(rest32, HALF, n, weight, rest[2 * n : 2 * n + 2])
-    send_rest(0)
-    for n in (2, 3):
-        pack_pairs(relays[n][0])
-        pack_pairs(owners[(n + 2) % 4][0])
-        send_pairs(n)
-    send_main(1)
-    send_rest(1)
+        if start == 0:
+            send_factors(part, rest32, me, 2, None, 2)
+
+    for step in range(8):
+        send_pairs(step)
+        if step < 4:
+            send_main(0, 16 * step, 16 * step + 16)
+        elif step < 6:
+            send_rest(0, 32 * (step - 4), 32 * (step - 3))
+        elif step == 6:
+            send_main(1, 0, 63)
+        else:
+            send_rest(1, 0, 63)
+        if step == 0:
+            for n in (2, 3):
+                pack_pairs(relays[n][0])
+                pack_pairs(owners[(n + 2) % 4][0])
+        if step == 1:
+            swap_rest.wait()
+            for n in range(11):
+                factors(rest32, HALF, n, weight, rest[2 * n : 2 * n + 2])
+        if step >= 2:
+            send_on(step - 2)
 
     def landed(part, n):
         b = (row // 2 + n) % 16
@@ -302,12 +312,10 @@
             ).start()
 
     pl.loop(0, 8)(take_first)
-    send_on(0)
-    send_on(1)
+    send_on(6)
     pl.loop(8, 16)(take_first)
+    send_on(7)
     send_products(0)
-    send_on(2)
-    send_on(3)
     pl.loop(0, 16)(take_second)
     send_products(1)
     send_products(2)
@@ -415,7 +423,7 @@
             pltpu.SemaphoreType.DMA((8,)),
             pltpu.SemaphoreType.DMA((8,)),
             pltpu.SemaphoreType.DMA((4,)),
-            pltpu.SemaphoreType.DMA((4,)),
+            pltpu.SemaphoreType.DMA((4, 2)),
             pltpu.SemaphoreType.DMA((3,)),
             pltpu.SemaphoreType.DMA((3,)),
             pltpu.SemaphoreType.DMA((3,)),

time: 83.9 us -> 76 us (0.906)
  Pallas kernels: 83.7 us -> 75.7 us
    pallas_call x1, Pallas kernels: 81.5 us -> 73.6 us  [fused(): pl.pallas_call(kernel, out_shape=jax.ShapeDtypeStruct((ROWS, COLS, 128),...]
where the time goes in v8:
time: 76 us; the launch traced here: 75.8 us
  Pallas kernels  75.7 us (100%)
    pallas_call x1, Pallas kernels, fused(): pl.pallas_call(kernel, out_shape=jax.ShapeDtypeStruct((ROWS, COLS, 128),...  73.6 us
    pallas_call x1, Pallas kernels, copy_out(): pl.pallas_call(copy_kernel, out_shape=jax.ShapeDtypeStruct(x.shape, x.dty...  2.19 us

profile of v8, /device:TPU:1, one launch (start us, length us, event | category | flops | bytes accessed | tf_op | source)
XLA Modules:
  0.0 75.8 jit_solution(15368620489406737914)
XLA Ops:
  0.0 73.6 %triangle_update.1.src_ref = bf16[22,176,128]{2,1,0:T(8,128)(2,1)} custom-call(bf16[22,176,128]{2,1,0:T(8,128)(2,1)} %own_ref.1, f32[1,128]{1,0:T(1,128)} %bitcast.2, bf16[128,512]{1,0:T(8,128)(2,1)} %weight_ref.1, bf16[128,128]{1,0:T(8,128)(2,1)} %gate_weight_ref.1, f32[1,128]{1,0:T(1,128)} %bitcast.3, bf16[128,128]{1,0:T(8,128)(2,1)} %out_weight_ref.1), custom_call_target="tpu_custom_call" | custom-call | tf_op jit(solution)/shard_map/triangle_update/pallas_call | solution.py:386
  73.6 2.2 %copy_out.1 = bf16[22,176,128]{2,1,0:T(8,128)(2,1)} custom-call(bf16[22,176,128]{2,1,0:T(8,128)(2,1)} %triangle_update.1.src_ref), custom_call_target="tpu_custom_call" | custom-call | tf_op jit(solution)/shard_map/copy_out/pallas_call | solution.py:452

commit v9 on v8

--- a/solution.py
+++ b/solution.py
@@ -74,9 +74,10 @@
 
 
 def kernel(
-    own_ref, gain_ref, weight_ref, gate_weight_ref, out_gain_ref, out_weight_ref, out_ref,
+    own_ref, gain_hbm, weight_hbm, gate_weight_hbm, out_gain_hbm, out_weight_hbm, out_ref,
+    gain_ref, weight_ref, gate_weight_ref, out_gain_ref, out_weight_ref,
     own, wt, main, rest, main32, rest32, g32, lr_a, lr_b, g, g_relay, lr_a_in, lr_b_in, g_in, left, right, p, p_in, p_sib, p32, gates, gains, ws, mixed, packed,
-    own_sem, map_send, map_recv, lr_send, lr_a_recv, lr_b_recv, g_send, g_recv, relay_send, relay_recv, p_send, p_recv, sib_send, sib_recv,
+    load_sems, map_send, map_recv, lr_send, lr_a_recv, lr_b_recv, g_send, g_recv, relay_send, relay_recv, p_send, p_recv, sib_send, sib_recv,
 ):
     row, col = place()
     half = col % 2
@@ -98,15 +99,30 @@
     forward = {"row": row + 4 - 8 * y_hi, "col": (col + 2) % 4}
     is_own = z == col
 
-    signal(sibling)
-    for hop in HOPS:
+    for hop in sorted(HOPS, key=lambda hop: -sum(min(v, 4 - v) for v in hop)):
         device, _ = chip_at(row, col, hop)
         signal(device)
         signal({"row": device["row"], "col": device["col"] + 1 - 2 * half})
-
-    own_copy = pltpu.make_async_copy(own_ref, own, own_sem)
-    own_copy.start()
-
+    signal(sibling)
+
+    loads = [
+        pltpu.make_async_copy(src, dst, load_sems.at[n])
+        for n, (src, dst) in enumerate(
+            (
+                (own_ref, own),
+                (gain_hbm, gain_ref),
+                (weight_hbm, weight_ref),
+                (gate_weight_hbm, gate_weight_ref),
+                (out_gain_hbm, out_gain_ref),
+                (out_weight_hbm, out_weight_ref),
+            )
+        )
+    ]
+    for load in loads:
+        load.start()
+
+    for load in loads[1:]:
+        load.wait()
     wt[...] = weight_ref[...].astype(F32).T
     parts = [wt[pl.ds(pl.multiple_of(128 * n + HALF * half, HALF), HALF), :] for n in range(4)]
     weight = jnp.concatenate(parts, axis=0).astype(BF16)
@@ -119,7 +135,7 @@
     for pad in (22, 23):
         g32[pl.ds(pad, COLS, stride=ROWS_PAD), :] = jnp.zeros((COLS, 128), F32)
 
-    own_copy.wait()
+    loads[0].wait()
 
     @pl.loop(0, 2)
     def _(n):
@@ -198,9 +214,6 @@
         pack_pairs(relays[n][0])
         pack_pairs(owners[(n + 2) % 4][0])
 
-    for n in range(11):
-        factors(main32, CHANNELS, n, weight_all, main[2 * n : 2 * n + 2])
-
     pl.semaphore_wait(barrier, 127)
 
     swap_rest = pltpu.make_async_remote_copy(
@@ -212,13 +225,22 @@
         device_id_type=MESH,
     )
     swap_rest.start()
-
-    parts = ((lr_a, lr_a_in, 0, 32, lr_a_recv), (lr_b, lr_b_in, 32, 16, lr_b_recv))
+    send_pairs(0)
+    send_pairs(1)
+    for n in (2, 3):
+        pack_pairs(relays[n][0])
+        pack_pairs(owners[(n + 2) % 4][0])
+
+    for n in range(11):
+        factors(main32, CHANNELS, n, weight_all, main[2 * n : 2 * n + 2])
+
+
+    parts = ((lr_a, lr_a_in, 0, 40, lr_a_recv), (lr_b, lr_b_in, 40, 8, lr_b_recv))
 
     def send_factors(part, source, channel, slot, device, kind):
         buffer, landing, start, rows, recv = parts[part]
         index = channel if kind < 2 else CHANNELS + channel
-        buffer[index] = source[pl.ds(pl.multiple_of(channel * 48 + start, 16), rows), :].astype(BF16)
+        buffer[index] = source[pl.ds(pl.multiple_of(channel * 48 + start, 8), rows), :].astype(BF16)
         if device is None:
             pltpu.make_async_copy(buffer.at[index], landing.at[me, slot], recv.at[row // 2]).start()
         else:
@@ -249,7 +271,8 @@
             send_factors(part, rest32, me, 2, None, 2)
 
     for step in range(8):
-        send_pairs(step)
+        if step >= 2:
+            send_pairs(step)
         if step < 4:
             send_main(0, 16 * step, 16 * step + 16)
         elif step < 6:
@@ -258,10 +281,6 @@
             send_main(1, 0, 63)
         else:
             send_rest(1, 0, 63)
-        if step == 0:
-            for n in (2, 3):
-                pack_pairs(relays[n][0])
-                pack_pairs(owners[(n + 2) % 4][0])
         if step == 1:
             swap_rest.wait()
             for n in range(11):
@@ -287,12 +306,12 @@
         for b, lanes, one, two in landed(0, n):
             rows = pl.ds(pl.multiple_of(48 * b, 48), 48)
             left[rows, lanes] = jnp.concatenate([one[:24], two[:24]], axis=0).astype(BF16)
-            take_right(b, 0, lanes, one[24:], two[24:])
+            take_right(b, 0, lanes, one[24:32], two[24:32])
+            take_right(b, 1, lanes, one[32:], two[32:])
 
     def take_second(n):
         for b, lanes, one, two in landed(1, n):
-            take_right(b, 1, lanes, one[:8], two[:8])
-            take_right(b, 2, lanes, one[8:], two[8:])
+            take_right(b, 2, lanes, one, two)
 
     def send_products(k):
         acc = lax.dot_general(right[256 * k : 256 * (k + 1), :], left[...], NT, preferred_element_type=F32)
@@ -316,8 +335,8 @@
     pl.loop(8, 16)(take_first)
     send_on(7)
     send_products(0)
+    send_products(1)
     pl.loop(0, 16)(take_second)
-    send_products(1)
     send_products(2)
 
     for s in range(8):
@@ -385,10 +404,15 @@
     vmem = pl.BlockSpec(memory_space=pltpu.VMEM)
     return pl.pallas_call(
         kernel,
-        out_shape=jax.ShapeDtypeStruct((ROWS, COLS, 128), BF16),
-        in_specs=[pl.BlockSpec(memory_space=pl.ANY)] + [vmem] * 5,
+        out_shape=pltpu.VMEM((ROWS, COLS, 128), BF16),
+        in_specs=[pl.BlockSpec(memory_space=pl.ANY)] * 6,
         out_specs=vmem,
         scratch_shapes=[
+            pltpu.VMEM((1, 128), F32),
+            pltpu.VMEM((128, 512), BF16),
+            pltpu.VMEM((128, 128), BF16),
+            pltpu.VMEM((1, 128), F32),
+            pltpu.VMEM((128, 128), BF16),
             pltpu.VMEM((ROWS, COLS, 128), BF16),
             pltpu.VMEM((512, 128), F32),
             pltpu.VMEM((ROWS, 128, 128), BF16),
@@ -396,12 +420,12 @@
             pltpu.VMEM((CHANNELS * 48, 128), F32),
             pltpu.VMEM((HALF * 48, 128), F32),
             pltpu.VMEM((COLS * ROWS_PAD, 128), F32),
-            pltpu.VMEM((CHANNELS + HALF, 32, 128), BF16),
-            pltpu.VMEM((CHANNELS + HALF, 16, 128), BF16),
+            pltpu.VMEM((CHANNELS + HALF, 40, 128), BF16),
+            pltpu.VMEM((CHANNELS + HALF, 8, 128), BF16),
             pltpu.VMEM((8, ROWS, ROWS_PAD, 128), BF16),
             pltpu.VMEM((4, ROWS, ROWS_PAD, 128), BF16),
-            pltpu.VMEM((64, 3, 32, 128), BF16),
-            pltpu.VMEM((64, 3, 16, 128), BF16),
+            pltpu.VMEM((64, 3, 40, 128), BF16),
+            pltpu.VMEM((64, 3, 8, 128), BF16),
             pltpu.VMEM((8, ROWS, ROWS_PAD, 128), BF16),
             pltpu.VMEM((768, 768), BF16),
             pltpu.VMEM((768, 768), BF16),
@@ -414,7 +438,7 @@
             pltpu.VMEM((128, 128), F32),
             pltpu.VMEM((8, 256, 128), F32),
             pltpu.VMEM((8, 184, 128), F32),
-            pltpu.SemaphoreType.DMA,
+            pltpu.SemaphoreType.DMA((6,)),
             pltpu.SemaphoreType.DMA,
             pltpu.SemaphoreType.DMA,
             pltpu.SemaphoreType.DMA((2,)),
@@ -436,15 +460,11 @@
     )(*args)
 
 
-def copy_kernel(src_ref, dst_ref, held, in_sems, out_sems):
-    ins = [pltpu.make_async_copy(src_ref.at[i], held.at[i], in_sems.at[i]) for i in range(ROWS)]
-    outs = [pltpu.make_async_copy(held.at[i], dst_ref.at[i], out_sems.at[i]) for i in range(ROWS)]
-    for copy in ins:
+def copy_kernel(src_ref, dst_ref, sems):
+    copies = [pltpu.make_async_copy(src_ref.at[i], dst_ref.at[i], sems.at[i]) for i in range(ROWS)]
+    for copy in copies:
         copy.start()
-    for i in range(ROWS):
-        ins[i].wait()
-        outs[i].start()
-    for copy in outs:
+    for copy in copies:
         copy.wait()
 
 
@@ -452,13 +472,9 @@
     return pl.pallas_call(
         copy_kernel,
         out_shape=jax.ShapeDtypeStruct(x.shape, x.dtype),
-        in_specs=[pl.BlockSpec(memory_space=pl.ANY)],
+        in_specs=[pl.BlockSpec(memory_space=pltpu.VMEM)],
         out_specs=pl.BlockSpec(memory_space=pl.ANY),
-        scratch_shapes=[
-            pltpu.VMEM(x.shape, x.dtype),
-            pltpu.SemaphoreType.DMA((ROWS,)),
-            pltpu.SemaphoreType.DMA((ROWS,)),
-        ],
+        scratch_shapes=[pltpu.SemaphoreType.DMA((ROWS,))],
         name="copy_out",
     )(x)
 

time: 76 us -> 77.2 us (1.016)
  local copies, waits for them, and re-layouts: 0 us -> 0.94 us
    unnamed x0 -> x2, local copies, waits for them, and re-layouts: none -> 0.94 us
where the time goes in v9:
time: 77.2 us; the launch traced here: 77.1 us
  Pallas kernels  76.1 us (99%)
  local copies, waits for them, and re-layouts  0.94 us (1%)
    pallas_call x1, Pallas kernels, fused(): pl.pallas_call(kernel, out_shape=pltpu.VMEM((ROWS, COLS, 128), BF16), in_...  73.8 us
    pallas_call x1, Pallas kernels, copy_out(): pl.pallas_call(copy_kernel, out_shape=jax.ShapeDtypeStruct(x.shape, x.dty...  2.33 us

profile of v9, /device:TPU:1, one launch (start us, length us, event | category | flops | bytes accessed | tf_op | source)
XLA Modules:
  0.0 77.1 jit_solution(11836028566512273949)
XLA Ops:
  0.0 73.8 %triangle_update.1.src_ref = bf16[22,176,128]{2,1,0:T(8,128)(2,1)S(1)} custom-call(bf16[22,176,128]{2,1,0:T(8,128)(2,1)} %own_ref.1, f32[1,128]{1,0:T(1,128)} %bitcast.2, bf16[128,512]{1,0:T(8,128)(2,1)} %weight_hbm.1, bf16[128,128]{1,0:T(8,128)(2,1)} %gate_weight_hbm.1, f32[1,128]{1,0:T(1,128)} %bitcast.3, bf16[128,128]{1,0:T(8,128)(2,1)} %out_weight_hbm.1), custom_call_target="tpu_custom_call" | custom-call | tf_op jit(solution)/shard_map/triangle_update/pallas_call | solution.py:405
  73.8 0.0 copy-start
  73.8 0.9 %copy-done = bf16[22,176,128]{2,1,0:T(8,128)(2,1)} copy-done((bf16[22,176,128]{2,1,0:T(8,128)(2,1)}, bf16[22,176,128]{2,1,0:T(8,128)(2,1)S(1)}, u32[]{:S(2)}) %copy-start) | copy-done | bytes 991256
  74.7 2.3 %copy_out.1 = bf16[22,176,128]{2,1,0:T(8,128)(2,1)} custom-call(bf16[22,176,128]{2,1,0:T(8,128)(2,1)} %copy-done), custom_call_target="tpu_custom_call" | custom-call | tf_op jit(solution)/shard_map/copy_out/pallas_call | solution.py:472
Async XLA Ops:
  73.8 1.0 %copy-start = (bf16[22,176,128]{2,1,0:T(8,128)(2,1)}, bf16[22,176,128]{2,1,0:T(8,128)(2,1)S(1)}, u32[]{:S(2)}) copy-start(bf16[22,176,128]{2,1,0:T(8,128)(2,1)S(1)} %triangle_update.1.src_ref) | copy-start | bytes 2973700

commit v10 on v9

--- a/solution.py
+++ b/solution.py
@@ -66,7 +66,15 @@
 
 
 HOPS = hop_order()
-GROUPS = ((0, 8), (8, 16), (16, 22))
+GROUPS = (
+    [(u, u) for u in range(8)],
+    [(u, 8 + u) for u in range(8)],
+    [(0, 18), (1, 19), (2, 20), (3, 21), (6, 16), (7, 17)],
+)
+
+
+def right_row(j):
+    return 24 + j if j < 16 else 6 + j if j < 18 else 22 + j
 
 
 def wait_bytes(ref, sem):
@@ -76,8 +84,8 @@
 def kernel(
     own_ref, gain_hbm, weight_hbm, gate_weight_hbm, out_gain_hbm, out_weight_hbm, out_ref,
     gain_ref, weight_ref, gate_weight_ref, out_gain_ref, out_weight_ref,
-    own, wt, main, rest, main32, rest32, g32, lr_a, lr_b, g, g_relay, lr_a_in, lr_b_in, g_in, left, right, p, p_in, p_sib, p32, gates, gains, ws, mixed, packed,
-    load_sems, map_send, map_recv, lr_send, lr_a_recv, lr_b_recv, g_send, g_recv, relay_send, relay_recv, p_send, p_recv, sib_send, sib_recv,
+    own, wt, main, rest, main32, rest32, g32, lr_a, lr_r, lr_b, g, g_relay, lr_a_in, lr_r_in, lr_b_in, g_in, left, right, p, p_in, p_sib, p32, gates, gains, ws, mixed, packed,
+    load_sems, map_send, map_recv, lr_send, lr_a_recv, lr_r_recv, lr_b_recv, g_send, g_recv, relay_send, relay_recv, p_send, p_recv, sib_send, sib_recv,
 ):
     row, col = place()
     half = col % 2
@@ -129,7 +137,7 @@
     weight_all = wt[...].astype(BF16)
     ones = jnp.full((128, 128), 1.0 / 128, BF16)
     rest[:, 96:128, :] = jnp.zeros((ROWS, 32, 128), BF16)
-    for pad in (22, 23, 46, 47):
+    for pad in (44, 45, 46, 47):
         main32[pl.ds(pad, CHANNELS, stride=48), :] = jnp.zeros((CHANNELS, 128), F32)
         rest32[pl.ds(pad, HALF, stride=48), :] = jnp.zeros((HALF, 128), F32)
     for pad in (22, 23):
@@ -156,7 +164,7 @@
         for u in range(2):
             lanes = slice(128 * u, 128 * (u + 1))
             target[pl.ds(2 * n + u, rows, stride=48), :] = one[:, lanes]
-            target[pl.ds(24 + 2 * n + u, rows, stride=48), :] = two[:, lanes]
+            target[pl.ds(right_row(2 * n + u), rows, stride=48), :] = two[:, lanes]
 
     def pack_pairs(v):
         for n in range(2):
@@ -235,52 +243,68 @@
         factors(main32, CHANNELS, n, weight_all, main[2 * n : 2 * n + 2])
 
 
-    parts = ((lr_a, lr_a_in, 0, 40, lr_a_recv), (lr_b, lr_b_in, 40, 8, lr_b_recv))
-
-    def send_factors(part, source, channel, slot, device, kind):
-        buffer, landing, start, rows, recv = parts[part]
-        index = channel if kind < 2 else CHANNELS + channel
-        buffer[index] = source[pl.ds(pl.multiple_of(channel * 48 + start, 8), rows), :].astype(BF16)
+    lane = lax.broadcasted_iota(jnp.int32, (8, 128), 1)
+    place8 = lax.broadcasted_iota(jnp.int32, (8, 128), 0)
+
+    def rows_of(source, channel, start, count):
+        return source[pl.ds(pl.multiple_of(channel * 48 + start, 8), count), :]
+
+    def send(buffer, index, target, recv, device, part):
         if device is None:
-            pltpu.make_async_copy(buffer.at[index], landing.at[me, slot], recv.at[row // 2]).start()
+            pltpu.make_async_copy(buffer.at[index], target, recv.at[row // 2]).start()
         else:
             pltpu.make_async_remote_copy(
                 src_ref=buffer.at[index],
-                dst_ref=landing.at[me, slot],
+                dst_ref=target,
                 send_sem=lr_send.at[part],
                 recv_sem=recv.at[row // 2],
                 device_id=device,
                 device_id_type=MESH,
             ).start()
 
-    def send_main(part, start, stop):
+    def send_first(chip, same, device):
+        channel = chip + (HALF * half if same else HALF - HALF * half)
+        lr_a[channel] = rows_of(main32, channel, 0, 40).astype(BF16)
+        send(lr_a, channel, lr_a_in.at[me, half], lr_a_recv, device, 0)
+
+    def send_rest(chip, device):
+        held = rows_of(rest32, chip, 0, 40)
+        full = [
+            jnp.where(lane < 96, held[8 * q : 8 * q + 8], pltpu.roll(held[32:40], 96 - 32 * q, 1)) for q in range(3)
+        ]
+        lr_r[chip] = jnp.concatenate(full + [held[24:32]], axis=0).astype(BF16)
+        send(lr_r, chip, lr_r_in.at[me], lr_r_recv, device, 1)
+
+    def send_second(chip, same, device):
+        channel = chip + (HALF * half if same else HALF - HALF * half)
+        held = rows_of(main32, channel, 40, 8)
+        if same:
+            held = jnp.where(place8 < 4, held, pltpu.roll(rows_of(rest32, chip, 40, 8), 4, 0))
+        lr_b[channel] = held.astype(BF16)
+        send(lr_b, channel, lr_b_in.at[me, half], lr_b_recv, device, 2)
+
+    def send_both(send_one, start, stop):
         for hop in HOPS[start:stop]:
             device, chip = chip_at(row, col, hop)
-            send_factors(part, main32, HALF * half + chip, half, device, 0)
-            across = {"row": device["row"], "col": device["col"] + 1 - 2 * half}
-            send_factors(part, main32, HALF - HALF * half + chip, half, across, 1)
+            send_one(chip, True, device)
+            send_one(chip, False, {"row": device["row"], "col": device["col"] + 1 - 2 * half})
         if start == 0:
-            send_factors(part, main32, HALF - HALF * half + me, half, sibling, 1)
-            send_factors(part, main32, HALF * half + me, half, None, 0)
-
-    def send_rest(part, start, stop):
-        for hop in HOPS[start:stop]:
-            device, chip = chip_at(row, col, hop)
-            send_factors(part, rest32, chip, 2, device, 2)
-        if start == 0:
-            send_factors(part, rest32, me, 2, None, 2)
+            send_one(me, False, sibling)
+            send_one(me, True, None)
 
     for step in range(8):
         if step >= 2:
             send_pairs(step)
         if step < 4:
-            send_main(0, 16 * step, 16 * step + 16)
+            send_both(send_first, 16 * step, 16 * step + 16)
         elif step < 6:
-            send_rest(0, 32 * (step - 4), 32 * (step - 3))
-        elif step == 6:
-            send_main(1, 0, 63)
+            for hop in HOPS[32 * (step - 4) : 32 * (step - 3)]:
+                device, chip = chip_at(row, col, hop)
+                send_rest(chip, device)
+            if step == 4:
+                send_rest(me, None)
         else:
-            send_rest(1, 0, 63)
+            send_both(send_second, 32 * (step - 6), 32 * (step - 5))
         if step == 1:
             swap_rest.wait()
             for n in range(11):
@@ -288,30 +312,52 @@
         if step >= 2:
             send_on(step - 2)
 
-    def landed(part, n):
+    def group(n):
         b = (row // 2 + n) % 16
-        landing, recv = parts[part][1], parts[part][4]
-        wait_bytes(landing.at[pl.ds(pl.multiple_of(4 * b, 4), 4)], recv.at[b])
-        for low in range(2):
-            for t in range(3):
-                one = landing[4 * b + low, t].astype(F32)
-                two = landing[4 * b + 2 + low, t].astype(F32)
-                yield b, slice(LANES * low + 128 * t, LANES * low + 128 * (t + 1)), one, two
+        return b, pl.ds(pl.multiple_of(4 * b, 4), 4)
 
     def take_right(b, k, lanes, one, two):
         rows = pl.ds(pl.multiple_of(256 * k + 16 * b, 16), 16)
         right[rows, lanes] = jnp.concatenate([one, two], axis=0).astype(BF16)
 
+    def tiles(b):
+        for low in range(2):
+            for t in range(3):
+                yield 4 * b + low, t, slice(LANES * low + 128 * t, LANES * low + 128 * (t + 1))
+
+    def first_rows(chip, t):
+        if t < 2:
+            return lr_a_in[chip, t].astype(F32)
+        held = lr_r_in[chip].astype(F32)
+        last = [pltpu.roll(held[8 * q : 8 * q + 8], 32 + 32 * q, 1) for q in range(3)]
+        last = jnp.where(lane < 32, last[0], jnp.where(lane < 64, last[1], last[2]))
+        rows = [held[8 * q : 8 * q + 8] for q in range(4)] + [last]
+        return jnp.concatenate([jnp.where(lane < 96, v, 0.0) for v in rows], axis=0)
+
+    def second_rows(chip, t):
+        if t < 2:
+            early, late = lr_a_in[chip, t, 16:32].astype(F32)[:8], lr_b_in[chip, t].astype(F32)
+        else:
+            early = jnp.where(lane < 96, lr_r_in[chip, 16:32].astype(F32)[:8], 0.0)
+            late = pltpu.roll(lr_b_in[chip, half].astype(F32), 4, 0)
+        return jnp.where(place8 < 6, late, early)
+
     def take_first(n):
-        for b, lanes, one, two in landed(0, n):
+        b, chips = group(n)
+        wait_bytes(lr_a_in.at[chips], lr_a_recv.at[b])
+        wait_bytes(lr_r_in.at[chips], lr_r_recv.at[b])
+        for chip, t, lanes in tiles(b):
+            one, two = first_rows(chip, t), first_rows(chip + 2, t)
             rows = pl.ds(pl.multiple_of(48 * b, 48), 48)
             left[rows, lanes] = jnp.concatenate([one[:24], two[:24]], axis=0).astype(BF16)
             take_right(b, 0, lanes, one[24:32], two[24:32])
             take_right(b, 1, lanes, one[32:], two[32:])
 
     def take_second(n):
-        for b, lanes, one, two in landed(1, n):
-            take_right(b, 2, lanes, one, two)
+        b, chips = group(n)
+        wait_bytes(lr_b_in.at[chips], lr_b_recv.at[b])
+        for chip, t, lanes in tiles(b):
+            take_right(b, 2, lanes, second_rows(chip, t), second_rows(chip + 2, t))
 
     def send_products(k):
         acc = lax.dot_general(right[256 * k : 256 * (k + 1), :], left[...], NT, preferred_element_type=F32)
@@ -357,7 +403,7 @@
     gain = jnp.concatenate([gain, gain], axis=1)
     out_weight = jnp.concatenate([ws[ours, :], ws[theirs, :]], axis=0).astype(BF16)
 
-    for k, (start, stop) in enumerate(GROUPS):
+    for k, members in enumerate(GROUPS):
         wait_bytes(p_in.at[k], p_recv.at[k])
         swap = pltpu.make_async_remote_copy(
             src_ref=p_in.at[k, :, :, pl.ds(pl.multiple_of(128 - 128 * half, 128), 256)],
@@ -374,8 +420,7 @@
         swap.wait()
         for t in range(2):
             p32[t, 512:1024, :] = p_sib[k, :, :, 128 * t : 128 * (t + 1)].astype(F32).reshape(512, 128)
-        for j in range(start, stop):
-            u = j - start
+        for u, j in members:
             q = jnp.concatenate([p32[t, pl.ds(u, CHANNELS, stride=8), :] for t in range(2)], axis=1)
             center = q - jnp.mean(q, axis=0, keepdims=True)
             spread = jnp.mean(center * center, axis=0, keepdims=True)
@@ -386,8 +431,9 @@
                 packed[u, 22 * s : 22 * s + 24, :] = update[24 * s : 24 * s + 24]
             out_ref[j] = packed[u, 0:COLS, :].astype(BF16)
 
-    wait_bytes(lr_a.at[pl.ds(0, 190)], lr_send.at[0])
-    wait_bytes(lr_b.at[pl.ds(0, 190)], lr_send.at[1])
+    wait_bytes(lr_a.at[pl.ds(0, 127)], lr_send.at[0])
+    wait_bytes(lr_r.at[pl.ds(0, 63)], lr_send.at[1])
+    wait_bytes(lr_b.at[pl.ds(0, 127)], lr_send.at[2])
     for k in range(3):
         wait_bytes(p.at[k, pl.ds(0, 63)], p_send.at[k])
     for v, _ in relays + owners[1:]:
@@ -420,12 +466,14 @@
             pltpu.VMEM((CHANNELS * 48, 128), F32),
             pltpu.VMEM((HALF * 48, 128), F32),
             pltpu.VMEM((COLS * ROWS_PAD, 128), F32),
-            pltpu.VMEM((CHANNELS + HALF, 40, 128), BF16),
-            pltpu.VMEM((CHANNELS + HALF, 8, 128), BF16),
+            pltpu.VMEM((CHANNELS, 40, 128), BF16),
+            pltpu.VMEM((HALF, 32, 128), BF16),
+            pltpu.VMEM((CHANNELS, 8, 128), BF16),
             pltpu.VMEM((8, ROWS, ROWS_PAD, 128), BF16),
             pltpu.VMEM((4, ROWS, ROWS_PAD, 128), BF16),
-            pltpu.VMEM((64, 3, 40, 128), BF16),
-            pltpu.VMEM((64, 3, 8, 128), BF16),
+            pltpu.VMEM((64, 2, 40, 128), BF16),
+            pltpu.VMEM((64, 32, 128), BF16),
+            pltpu.VMEM((64, 2, 8, 128), BF16),
             pltpu.VMEM((8, ROWS, ROWS_PAD, 128), BF16),
             pltpu.VMEM((768, 768), BF16),
             pltpu.VMEM((768, 768), BF16),
@@ -441,7 +489,8 @@
             pltpu.SemaphoreType.DMA((6,)),
             pltpu.SemaphoreType.DMA,
             pltpu.SemaphoreType.DMA,
-            pltpu.SemaphoreType.DMA((2,)),
+            pltpu.SemaphoreType.DMA((3,)),
+            pltpu.SemaphoreType.DMA((16,)),
             pltpu.SemaphoreType.DMA((16,)),
             pltpu.SemaphoreType.DMA((16,)),
             pltpu.SemaphoreType.DMA((8,)),
@@ -476,7 +525,7 @@
         out_specs=pl.BlockSpec(memory_space=pl.ANY),
         scratch_shapes=[pltpu.SemaphoreType.DMA((ROWS,))],
         name="copy_out",
-    )(x)
+    )(pltpu.with_memory_space_constraint(x, pltpu.VMEM))
 
 
 def body(pair_map, in_gain, project_weight, gate_weight, out_gain, out_weight):

time: 77.2 us -> 72.2 us (0.935)
  Pallas kernels: 76.1 us -> 72.1 us
  local copies, waits for them, and re-layouts: 0.94 us -> 0 us
    pallas_call x1, Pallas kernels: 73.8 us -> 71 us  [fused(): pl.pallas_call(kernel, out_shape=pltpu.VMEM((ROWS, COLS, 128), BF16), in_...]
    pallas_call x1, Pallas kernels: 2.33 us -> 1.13 us  [copy_out(): pl.pallas_call(copy_kernel, out_shape=jax.ShapeDtypeStruct(x.shape, x.dty...]
    unnamed x2 -> x0, local copies, waits for them, and re-layouts: 0.94 us -> none
where the time goes in v10:
time: 72.2 us; the launch traced here: 72.1 us
  Pallas kernels  72.1 us (100%)
    pallas_call x1, Pallas kernels, fused(): pl.pallas_call(kernel, out_shape=pltpu.VMEM((ROWS, COLS, 128), BF16), in_...  71 us

profile of v10, /device:TPU:1, one launch (start us, length us, event | category | flops | bytes accessed | tf_op | source)
XLA Modules:
  0.0 72.1 jit_solution(247782645710519003)
XLA Ops:
  0.0 71.0 %triangle_update.1.src_ref = bf16[22,176,128]{2,1,0:T(8,128)(2,1)S(1)} custom-call(bf16[22,176,128]{2,1,0:T(8,128)(2,1)} %own_ref.1, f32[1,128]{1,0:T(1,128)} %bitcast.2, bf16[128,512]{1,0:T(8,128)(2,1)} %weight_hbm.1, bf16[128,128]{1,0:T(8,128)(2,1)} %gate_weight_hbm.1, f32[1,128]{1,0:T(1,128)} %bitcast.3, bf16[128,128]{1,0:T(8,128)(2,1)} %out_weight_hbm.1), custom_call_target="tpu_custom_call" | custom-call | tf_op jit(solution)/shard_map/triangle_update/pallas_call | solution.py:451
  71.0 1.1 %copy_out.1 = bf16[22,176,128]{2,1,0:T(8,128)(2,1)} custom-call(bf16[22,176,128]{2,1,0:T(8,128)(2,1)S(1)} %triangle_update.1.src_ref), custom_call_target="tpu_custom_call" | custom-call | tf_op jit(solution)/shard_map/copy_out/pallas_call | solution.py:521

commit v11 on v10

--- a/solution.py
+++ b/solution.py
@@ -41,31 +41,12 @@
     return {"row": row2, "col": low * 2 + col % 2}, row2 * 2 + low
 
 
-def hop_order():
-    left = [(a, b, c) for a in range(4) for b in range(4) for c in range(4)][1:]
-    use = [0] * 6
-    order = []
-
-    def after(hop):
-        then = list(use)
-        for axis, step in enumerate(hop):
-            then[2 * axis] += (0, 2, 2, 0)[step]
-            then[2 * axis + 1] += (0, 0, 2, 2)[step]
-        return then
-
-    def score(hop):
-        then = after(hop)
-        return max(then) - min(then), sum(v * v for v in then), (hop[0] * 37 + hop[1] * 11 + hop[2] * 5) % 17
-
-    while left:
-        best = min(left, key=score)
-        use = after(best)
-        left.remove(best)
-        order.append(best)
-    return order
-
-
-HOPS = hop_order()
+HOP_ORDER = (
+    42, 4, 46, 58, 16, 1, 43, 41, 3, 48, 26, 12, 38, 54, 28, 34, 8, 59, 17, 45, 7,
+    30, 52, 47, 5, 13, 39, 62, 20, 2, 40, 15, 37, 22, 60, 10, 32, 19, 57, 51, 25, 27,
+    49, 61, 23, 6, 44, 50, 24, 29, 55, 18, 56, 63, 21, 11, 33, 36, 14, 53, 31, 35, 9,
+)
+HOPS = [(n // 16, n // 4 % 4, n % 4) for n in HOP_ORDER]
 GROUPS = (
     [(u, u) for u in range(8)],
     [(u, 8 + u) for u in range(8)],
@@ -309,8 +290,8 @@
             swap_rest.wait()
             for n in range(11):
                 factors(rest32, HALF, n, weight, rest[2 * n : 2 * n + 2])
-        if step >= 2:
-            send_on(step - 2)
+        if step >= 1:
+            send_on(step - 1)
 
     def group(n):
         b = (row // 2 + n) % 16
@@ -377,9 +358,8 @@
             ).start()
 
     pl.loop(0, 8)(take_first)
-    send_on(6)
+    send_on(7)
     pl.loop(8, 16)(take_first)
-    send_on(7)
     send_products(0)
     send_products(1)
     pl.loop(0, 16)(take_second)

time: 72.2 us -> 70.9 us (0.982); the launches traced: 72.1 us -> 69.8 us
  Pallas kernels: 72.1 us -> 69.8 us
    pallas_call x1, Pallas kernels: 71 us -> 68.7 us  [fused(): pl.pallas_call(kernel, out_shape=pltpu.VMEM((ROWS, COLS, 128), BF16), in_...]
where the time goes in v11:
time: 70.9 us; the launch traced here: 69.8 us
  Pallas kernels  69.8 us (98%)
    pallas_call x1, Pallas kernels, fused(): pl.pallas_call(kernel, out_shape=pltpu.VMEM((ROWS, COLS, 128), BF16), in_...  68.7 us

profile of v11, /device:TPU:1, one launch (start us, length us, event | category | flops | bytes accessed | tf_op | source)
XLA Modules:
  0.0 69.8 jit_solution(4866126481800836256)
XLA Ops:
  0.0 68.7 %triangle_update.1.src_ref = bf16[22,176,128]{2,1,0:T(8,128)(2,1)S(1)} custom-call(bf16[22,176,128]{2,1,0:T(8,128)(2,1)} %own_ref.1, f32[1,128]{1,0:T(1,128)} %bitcast.2, bf16[128,512]{1,0:T(8,128)(2,1)} %weight_hbm.1, bf16[128,128]{1,0:T(8,128)(2,1)} %gate_weight_hbm.1, f32[1,128]{1,0:T(1,128)} %bitcast.3, bf16[128,128]{1,0:T(8,128)(2,1)} %out_weight_hbm.1), custom_call_target="tpu_custom_call" | custom-call | tf_op jit(solution)/shard_map/triangle_update/pallas_call | solution.py:431
  68.7 1.1 %copy_out.1 = bf16[22,176,128]{2,1,0:T(8,128)(2,1)} custom-call(bf16[22,176,128]{2,1,0:T(8,128)(2,1)S(1)} %triangle_update.1.src_ref), custom_call_target="tpu_custom_call" | custom-call | tf_op jit(solution)/shard_map/copy_out/pallas_call | solution.py:501

commit v12 on v11

--- a/solution.py
+++ b/solution.py
@@ -274,8 +274,10 @@
             send_one(me, True, None)
 
     for step in range(8):
-        if step >= 2:
+        if 2 <= step < 7:
             send_pairs(step)
+        if step == 6:
+            send_pairs(7)
         if step < 4:
             send_both(send_first, 16 * step, 16 * step + 16)
         elif step < 6:
@@ -292,6 +294,8 @@
                 factors(rest32, HALF, n, weight, rest[2 * n : 2 * n + 2])
         if step >= 1:
             send_on(step - 1)
+        if step == 7:
+            send_on(7)
 
     def group(n):
         b = (row // 2 + n) % 16
@@ -357,9 +361,7 @@
                 device_id_type=MESH,
             ).start()
 
-    pl.loop(0, 8)(take_first)
-    send_on(7)
-    pl.loop(8, 16)(take_first)
+    pl.loop(0, 16)(take_first)
     send_products(0)
     send_products(1)
     pl.loop(0, 16)(take_second)

time: 70.9 us -> 70.3 us (level); the launches traced: 69.8 us -> 70.2 us
  no operation moved by 1% of the time
where the time goes in v12:
time: 70.3 us; the launch traced here: 70.2 us
  Pallas kernels  70.2 us (100%)
    pallas_call x1, Pallas kernels, fused(): pl.pallas_call(kernel, out_shape=pltpu.VMEM((ROWS, COLS, 128), BF16), in_...  69 us

profile of v12, /device:TPU:1, one launch (start us, length us, event | category | flops | bytes accessed | tf_op | source)
XLA Modules:
  0.0 70.2 jit_solution(17604299624716270024)
XLA Ops:
  0.0 69.0 %triangle_update.1.src_ref = bf16[22,176,128]{2,1,0:T(8,128)(2,1)S(1)} custom-call(bf16[22,176,128]{2,1,0:T(8,128)(2,1)} %own_ref.1, f32[1,128]{1,0:T(1,128)} %bitcast.2, bf16[128,512]{1,0:T(8,128)(2,1)} %weight_hbm.1, bf16[128,128]{1,0:T(8,128)(2,1)} %gate_weight_hbm.1, f32[1,128]{1,0:T(1,128)} %bitcast.3, bf16[128,128]{1,0:T(8,128)(2,1)} %out_weight_hbm.1), custom_call_target="tpu_custom_call" | custom-call | tf_op jit(solution)/shard_map/triangle_update/pallas_call | solution.py:433
  69.1 1.1 %copy_out.1 = bf16[22,176,128]{2,1,0:T(8,128)(2,1)} custom-call(bf16[22,176,128]{2,1,0:T(8,128)(2,1)S(1)} %triangle_update.1.src_ref), custom_call_target="tpu_custom_call" | custom-call | tf_op jit(solution)/shard_map/copy_out/pallas_call | solution.py:503

commit v13 on v12

--- a/solution.py
+++ b/solution.py
@@ -445,9 +445,9 @@
             pltpu.VMEM((512, 128), F32),
             pltpu.VMEM((ROWS, 128, 128), BF16),
             pltpu.VMEM((ROWS, 128, 128), BF16),
-            pltpu.VMEM((CHANNELS * 48, 128), F32),
-            pltpu.VMEM((HALF * 48, 128), F32),
-            pltpu.VMEM((COLS * ROWS_PAD, 128), F32),
+            pltpu.VMEM((CHANNELS * 48 + 48, 128), F32),
+            pltpu.VMEM((HALF * 48 + 48, 128), F32),
+            pltpu.VMEM((COLS * ROWS_PAD + ROWS_PAD, 128), F32),
             pltpu.VMEM((CHANNELS, 40, 128), BF16),
             pltpu.VMEM((HALF, 32, 128), BF16),
             pltpu.VMEM((CHANNELS, 8, 128), BF16),
@@ -462,7 +462,7 @@
             pltpu.VMEM((3, 64, 8, LANES), BF16),
             pltpu.VMEM((3, 64, 8, LANES), BF16),
             pltpu.VMEM((3, 64, 8, 256), BF16),
-            pltpu.VMEM((2, CHANNELS * 8, 128), F32),
+            pltpu.VMEM((2, CHANNELS * 8 + 8, 128), F32),
             pltpu.VMEM((ROWS, 192, 128), F32),
             pltpu.VMEM((128, 128), F32),
             pltpu.VMEM((128, 128), F32),

time: 70.3 us -> 70.3 us (level)
  no operation moved by 1% of the time
where the time goes in v13:
time: 70.3 us; the launch traced here: 70.2 us
  Pallas kernels  70.2 us (100%)
    pallas_call x1, Pallas kernels, fused(): pl.pallas_call(kernel, out_shape=pltpu.VMEM((ROWS, COLS, 128), BF16), in_...  69.1 us

profile of v13, /device:TPU:1, one launch (start us, length us, event | category | flops | bytes accessed | tf_op | source)
XLA Modules:
  0.0 70.2 jit_solution(4631536167750857658)
XLA Ops:
  0.0 69.1 %triangle_update.1.src_ref = bf16[22,176,128]{2,1,0:T(8,128)(2,1)S(1)} custom-call(bf16[22,176,128]{2,1,0:T(8,128)(2,1)} %own_ref.1, f32[1,128]{1,0:T(1,128)} %bitcast.2, bf16[128,512]{1,0:T(8,128)(2,1)} %weight_hbm.1, bf16[128,128]{1,0:T(8,128)(2,1)} %gate_weight_hbm.1, f32[1,128]{1,0:T(1,128)} %bitcast.3, bf16[128,128]{1,0:T(8,128)(2,1)} %out_weight_hbm.1), custom_call_target="tpu_custom_call" | custom-call | tf_op jit(solution)/shard_map/triangle_update/pallas_call | solution.py:433
  69.1 1.1 %copy_out.1 = bf16[22,176,128]{2,1,0:T(8,128)(2,1)} custom-call(bf16[22,176,128]{2,1,0:T(8,128)(2,1)S(1)} %triangle_update.1.src_ref), custom_call_target="tpu_custom_call" | custom-call | tf_op jit(solution)/shard_map/copy_out/pallas_call | solution.py:503
